TPU v7x, 512 devices: a whole 4x4x16 slice. The times are simulated.
512 devices in a mesh: section: 2 (over x_hi), gy: 16 (over y, x_lo, core), gx: 16 (over z).
Axes of the slice: x: 4 (x_hi: 2, x_lo: 2; x = x_hi * 2 + x_lo), y: 4, z: 16, core: 2. Of those that a mesh axis runs over, the one named last changes fastest.
Arguments:
- images: bfloat16 [2, 512, 1024, 128], P('section', 'gy', 'gx'), may hold values from -6 to 6
- first_kernel: bfloat16 [3, 3, 128, 128], replicated, may hold values from -0.1875 to 0.1875
- projection: bfloat16 [128, 256], replicated, may hold values from -0.5 to 0.5
- second_kernel: bfloat16 [3, 3, 256, 256], replicated, may hold values from -0.125 to 0.125
- cotangent: bfloat16 [2, 256, 512, 256], P('section', 'gy', 'gx'), may hold values from -0.15625 to 0.15625
Outputs:
- features: bfloat16 [2, 256, 512, 256], P('section', 'gy', 'gx')
- grad_first: float32 [3, 3, 128, 128], replicated
- grad_projection: float32 [128, 256], replicated
- grad_second: float32 [3, 3, 256, 256], replicated
All inputs are finite; a program needn't handle non-finite values.
Results may differ from a plain program's by a relative error of at most 0.014.
Values may be sent and summed in bfloat16 or wider, within the bound.
A program may use at most 64 MiB of HBM per device.

v0:
```python
import jax
import jax.numpy as jnp
from jax import lax
from jax.sharding import PartitionSpec as P


def padded_2(array, sides, width):
    for axis, dim in sides:
        size, length = (lax.axis_size(axis), array.shape[dim])
        up = [(i, (i + 1) % size) for i in range(size - 1)]
        down = [(j, i) for i, j in up]
        last = lax.slice_in_dim(array, length - width, length, axis=dim)
        initial = lax.slice_in_dim(array, 0, width, axis=dim)
        before = lax.ppermute(last, axis, up)
        after = lax.ppermute(initial, axis, down)
        array = jnp.concatenate([before, array, after], axis=dim)
    return array


def from_partner(block, axis, bit):
    count = lax.axis_size(axis)
    route = []
    for low in range(count):
        high = low | 1 << bit
        if high != low and high < count:
            route += [(low, high), (high, low)]
    return lax.ppermute(block, axis, route)


def silu_slope(values):
    sigma = jax.nn.sigmoid(values)
    return sigma * (1.0 + values * (1.0 - sigma))


def conv_forward(padded, kernel, row_count, col_count):
    total = jnp.zeros((row_count * col_count, kernel.shape[3]), jnp.float32)
    for row_tap in range(3):
        for col_tap in range(3):
            piece = padded[row_tap : row_tap + row_count, col_tap : col_tap + col_count].reshape(
                row_count * col_count, padded.shape[2]
            )
            total = total + jnp.dot(
                piece, kernel[row_tap, col_tap], preferred_element_type=jnp.float32
            )
    return total


def conv_slopes(padded, slope, row_count, col_count):
    pieces = []
    for row_tap in range(3):
        for col_tap in range(3):
            piece = padded[row_tap : row_tap + row_count, col_tap : col_tap + col_count].reshape(
                row_count * col_count, padded.shape[2]
            )
            pieces.append(jnp.einsum("pc,pd->cd", piece, slope, preferred_element_type=jnp.float32))
    return jnp.stack(pieces).reshape(3, 3, padded.shape[2], slope.shape[1])


def conv_back(padded, kernel, row_count, col_count):
    total = jnp.zeros((row_count * col_count, kernel.shape[2]), jnp.float32)
    for row_tap in range(3):
        for col_tap in range(3):
            piece = padded[
                2 - row_tap : 2 - row_tap + row_count, 2 - col_tap : 2 - col_tap + col_count
            ].reshape(row_count * col_count, padded.shape[2])
            total = total + jnp.einsum(
                "pd,cd->pc", piece, kernel[row_tap, col_tap], preferred_element_type=jnp.float32
            )
    return total


def first_forward(tile, first_kernel):
    row_count, col_count, channels = tile.shape
    padded = padded_2(tile, (("gy", 0), ("gx", 1)), 1)
    before = conv_forward(padded, first_kernel, row_count, col_count)
    hidden = jax.nn.silu(before).astype(jnp.bfloat16).reshape(row_count, col_count, channels)
    pooled = (
        hidden.astype(jnp.float32)
        .reshape(row_count // 2, 2, col_count // 2, 2, channels)
        .sum(axis=(1, 3))
        * 0.25
    ).astype(jnp.bfloat16)
    return (padded, before, pooled)


def project(pooled, projection):
    half_rows, half_cols, channels = pooled.shape
    flat = jnp.dot(
        pooled.reshape(half_rows * half_cols, channels),
        projection,
        preferred_element_type=jnp.float32,
    )
    return flat.astype(jnp.bfloat16).reshape(half_rows, half_cols, projection.shape[1])


def second_pass(middle, second_kernel, upstream):
    half_rows, half_cols, wide = middle.shape
    padded = padded_2(middle, (("gy", 0), ("gx", 1)), 1)
    before = conv_forward(padded, second_kernel, half_rows, half_cols)
    output = jax.nn.silu(before).astype(jnp.bfloat16).reshape(half_rows, half_cols, wide)
    flat_up = upstream.reshape(half_rows * half_cols, wide).astype(jnp.float32)
    slope = (flat_up * silu_slope(before)).astype(jnp.bfloat16)
    kernel_grad = conv_slopes(padded, slope, half_rows, half_cols)
    slope_padded = padded_2(slope.reshape(half_rows, half_cols, wide), (("gy", 0), ("gx", 1)), 1)
    back = conv_back(slope_padded, second_kernel, half_rows, half_cols).astype(jnp.bfloat16)
    return (output, kernel_grad, back.reshape(half_rows, half_cols, wide))


def projection_back(pooled, back, projection):
    half_rows, half_cols, channels = pooled.shape
    flat_pool = pooled.reshape(half_rows * half_cols, channels)
    flat_back = back.reshape(half_rows * half_cols, back.shape[2])
    grad = jnp.einsum("pc,pd->cd", flat_pool, flat_back, preferred_element_type=jnp.float32)
    pooled_slope = jnp.einsum(
        "pd,cd->pc", flat_back, projection, preferred_element_type=jnp.float32
    )
    return (grad, pooled_slope.astype(jnp.bfloat16).reshape(half_rows, half_cols, channels))


def first_back(padded, before, pooled_slope):
    half_rows, half_cols, channels = pooled_slope.shape
    spread = jnp.broadcast_to(
        (pooled_slope.astype(jnp.float32) * 0.25)[:, None, :, None, :],
        (half_rows, 2, half_cols, 2, channels),
    )
    spread = spread.reshape(4 * half_rows * half_cols, channels)
    slope = (spread * silu_slope(before)).astype(jnp.bfloat16)
    return conv_slopes(padded, slope, 2 * half_rows, 2 * half_cols)


def per_device(images, first_kernel, projection, second_kernel, cotangent):
    padded, before, pooled = first_forward(images[0], first_kernel)
    middle = from_partner(project(pooled, projection), "section", 0)
    output, grad_second, back_far = second_pass(middle, second_kernel, cotangent[0])
    back = from_partner(back_far, "section", 0)
    grad_projection, pooled_slope = projection_back(pooled, back, projection)
    grad_first = first_back(padded, before, pooled_slope)
    grad_first, grad_projection, grad_second = lax.psum(
        (grad_first, grad_projection, grad_second), ("section", "gy", "gx")
    )
    return (output[None], grad_first, grad_projection, grad_second)


def solution(mesh):
    placed = (P("section", "gy", "gx", None), P(), P(), P(), P("section", "gy", "gx", None))
    return jax.shard_map(
        per_device,
        mesh=mesh,
        in_specs=placed,
        out_specs=(P("section", "gy", "gx", None), P(), P(), P()),
        check_vma=False,
    )
```

profile of v0, /device:TPU:1, one launch (start us, length us, event | category | flops | bytes accessed | tf_op | source)
XLA Modules:
  0.0 603.9 jit_solution(15916452577856336045)
XLA Ops:
  7.2 0.8 slice_bitcast_fusion.3
  8.0 4.5 collective-permute-start
  12.5 5.6 collective-permute-start.1
  18.1 0.8 collective-permute-done.1
  18.9 0.9 pad_maximum_fusion.15
  19.8 2.2 collective-permute-start.2
  22.1 1.4 collective-permute-start.3
  23.5 1.3 pad_maximum_fusion.1
  24.8 0.3 fusion.81
  25.1 1.8 collective-permute-done.3
  26.9 0.3 maximum_maximum_fusion
  27.2 0.6 fusion.93
  27.8 0.3 fusion.73
  28.1 0.3 convolution_add_fusion.6
  28.4 0.3 convolution_add_fusion.5
  28.7 0.3 convolution_add_fusion.4
  29.0 0.3 convolution_add_fusion.3
  29.3 0.3 convolution_add_fusion.2
  29.6 0.3 convolution_add_fusion.1
  29.8 0.5 multiply_convert_fusion.1
  30.3 0.9 convert_reduce_fusion
  31.5 4.5 collective-permute-start.4
  36.0 6.5 %collective-permute-done.4 = bf16[16,32,256]{2,1,0:T(8,128)(2,1)S(1)} collective-permute-done((bf16[16,32,256]{2,1,0:T(8,128)(2,1)S(1)}, bf16[16,32,256]{2,1,0:T(8,128)(2,1)S(1)}, u32[]{:S(2)}, u32[]{:S(2)}) %collective-permute-start.4) | collective-permute-done | bytes 262176 | tf_op jit(solution)/shard_map/ppermute | solution.py:27
  42.5 4.5 collective-permute-start.5
  47.0 1.9 collective-permute-start.6
  49.0 3.1 collective-permute-done.6
  52.2 3.6 collective-permute-start.7
  55.8 1.3 collective-permute-start.8
  57.6 4.0 collective-permute-done.8
  61.6 0.4 pad_maximum_fusion.8
  63.4 0.7 copy-done.7
  64.1 1.1 fusion.26
  65.5 3.1 collective-permute-start.9
  68.6 1.9 collective-permute-start.10
  70.5 0.3 fusion.13
  70.8 0.3 fusion.12
  71.1 0.3 fusion.11
  71.4 0.3 fusion.10
  71.6 0.3 fusion.9
  71.9 0.3 fusion.8
  72.2 1.4 collective-permute-done.10
  73.7 1.3 collective-permute-start.11
  75.0 5.7 collective-permute-start.12
  81.0 0.5 collective-permute-done.12
  84.1 4.3 collective-permute-start.13
  88.4 0.3 fusion.7
  88.7 0.3 fusion.6
  89.0 5.9 collective-permute-done.13
  95.2 0.5 broadcast_in_dim.2
  95.6 0.4 multiply_convert_fusion
  96.1 0.3 fusion.25
  96.4 0.4 fusion.24
  96.8 0.4 fusion.23
  97.1 0.4 fusion.22
  97.5 0.3 fusion.21
  97.8 0.4 fusion.20
  98.2 0.4 fusion.19
  98.6 0.4 fusion.18
  98.9 0.4 fusion.17
  99.3 0.9 convolution_bitcast_fusion.9
  100.2 491.1 %all-reduce.3.cloned.1.call-done = (f32[3,3,128,128]{3,2,1,0:T(8,128)}, f32[128,256]{1,0:T(8,128)}, f32[3,3,256,256]{3,2,1,0:T(8,128)}) async-done(((f32[3,3,128,128]{3,2,1,0:T(8,128)}, f32[128,256]{1,0:T(8,128)}, f32[3,3,256,256]{3,2,1,0:T(8,128)}), (f32[3,3,128,128]{3,2,1,0:T(8,128)}, f32[128,256]{1,0:T(8,128)}, f32[3,3,256,256]{3,2,1,0:T(8,128)})) %all-reduce.3.cloned.1.call-update) | async-done | bytes 3080208 | tf_op jit(solution)/shard_map/psum | solution.py:138
  591.3 2.0 copy.32
  593.2 0.7 copy.33
  593.9 3.2 copy.34
  (55 shorter events, 5.6 us)
Async XLA Ops:
  7.2 24.1 %copy-start = (bf16[128,256]{1,0:T(8,128)(2,1)S(1)}, bf16[128,256]{1,0:T(8,128)(2,1)}, u32[]{:S(2)}) copy-start(bf16[128,256]{1,0:T(8,128)(2,1)} %param.7) | copy-start | bytes 196612
  7.2 17.6 %copy-start.5 = (bf16[3,3,128,128]{3,2,1,0:T(8,128)(2,1)S(1)}, bf16[3,3,128,128]{3,2,1,0:T(8,128)(2,1)}, u32[]{:S(2)}) copy-start(bf16[3,3,128,128]{3,2,1,0:T(8,128)(2,1)} %param.6) | copy-start | bytes 884740
  7.2 584.1 %all-reduce.3.cloned.1.call-start = ((), (), s32[]{:S(2)}) async-start(), calls=%async_computation | async-start | bytes 6160384 | tf_op jit(solution)/shard_map/psum | solution.py:138
  8.0 10.1 %collective-permute-start = (bf16[1,64,128]{2,1,0:T(8,128)(2,1)S(1)}, bf16[1,64,128]{2,1,0:T(8,128)(2,1)S(1)}, u32[]{:S(2)}, u32[]{:S(2)}) collective-permute-start(bf16[1,64,128]{2,1,0:T(8,128)(2,1)S(1)} %get-tuple-element.21), channel_id=1, source_target_pairs={{0,16},{16,32},{32,48},{48,64},{64,80},{80,96},{96,112},{112,128},... | collective-permute-start | bytes 49160 | tf_op jit(solution)/shard_map/ppermute | solution.py:14
  12.5 6.4 %collective-permute-start.1 = (bf16[1,64,128]{2,1,0:T(8,128)(2,1)S(1)}, bf16[1,64,128]{2,1,0:T(8,128)(2,1)S(1)}, u32[]{:S(2)}, u32[]{:S(2)}) collective-permute-start(bf16[1,64,128]{2,1,0:T(8,128)(2,1)S(1)} %get-tuple-element.22), channel_id=1, source_target_pairs={{16,0},{32,16},{48,32},{64,48},{80,64},{96,80},{112,96},{128,112},... | collective-permute-start | bytes 49160 | tf_op jit(solution)/shard_map/ppermute | solution.py:15
  19.8 5.2 collective-permute-start.2
  22.1 4.8 copy-start.1
  22.1 4.8 collective-permute-start.3
  31.2 25.9 %copy-start.2 = (bf16[3,3,256,256]{3,2,1,0:T(8,128)(2,1)S(1)}, bf16[3,3,256,256]{3,2,1,0:T(8,128)(2,1)}, u32[]{:S(2)}) copy-start(bf16[3,3,256,256]{3,2,1,0:T(8,128)(2,1)} %param.8) | copy-start | bytes 3538948
  31.5 11.0 %collective-permute-start.4 = (bf16[16,32,256]{2,1,0:T(8,128)(2,1)S(1)}, bf16[16,32,256]{2,1,0:T(8,128)(2,1)S(1)}, u32[]{:S(2)}, u32[]{:S(2)}) collective-permute-start(bf16[16,32,256]{2,1,0:T(8,128)(2,1)S(1)} %bitcast.328), channel_id=1, source_target_pairs={{0,256},{256,0},{1,257},{257,1},{2,258},{258,2},{3,259},{259,3},{4... | collective-permute-start | bytes 786440 | tf_op jit(solution)/shard_map/ppermute | solution.py:27
  42.5 6.5 %collective-permute-start.5 = (bf16[1,32,256]{2,1,0:T(8,128)(2,1)S(1)}, bf16[1,32,256]{2,1,0:T(8,128)(2,1)S(1)}, u32[]{:S(2)}, u32[]{:S(2)}) collective-permute-start(bf16[1,32,256]{2,1,0:T(8,128)(2,1)S(1)} %get-tuple-element.52), channel_id=1, source_target_pairs={{0,16},{16,32},{32,48},{48,64},{64,80},{80,96},{96,112},{112,128},... | collective-permute-start | bytes 49160 | tf_op jit(solution)/shard_map/ppermute | solution.py:14
  47.0 5.1 collective-permute-start.6
  52.2 5.3 collective-permute-start.7
  55.8 5.8 collective-permute-start.8
  63.1 1.0 copy-start.7
  65.5 6.7 %collective-permute-start.9 = (bf16[1,32,256]{2,1,0:T(8,128)(2,1)S(1)}, bf16[1,32,256]{2,1,0:T(8,128)(2,1)S(1)}, u32[]{:S(2)}, u32[]{:S(2)}) collective-permute-start(bf16[1,32,256]{2,1,0:T(8,128)(2,1)S(1)} %get-tuple-element.46), channel_id=1, source_target_pairs={{0,16},{16,32},{32,48},{48,64},{64,80},{80,96},{96,112},{112,128},... | collective-permute-start | bytes 49160 | tf_op jit(solution)/shard_map/ppermute | solution.py:14
  68.6 5.1 collective-permute-start.10
  73.7 7.3 %collective-permute-start.11 = (bf16[18,1,256]{2,1,0:T(2,128)(2,1)S(1)}, bf16[18,1,256]{2,1,0:T(2,128)(2,1)S(1)}, u32[]{:S(2)}, u32[]{:S(2)}) collective-permute-start(bf16[18,1,256]{2,1,0:T(2,128)(2,1)S(1)} %get-tuple-element.37), channel_id=1, source_target_pairs={{1,0},{2,1},{3,2},{4,3},{5,4},{6,5},{7,6},{8,7},{9,8},{10,9},{11,1... | collective-permute-start | bytes 27656 | tf_op jit(solution)/shard_map/ppermute | solution.py:15
  75.0 6.6 %collective-permute-start.12 = (bf16[18,1,256]{2,1,0:T(2,128)(2,1)S(1)}, bf16[18,1,256]{2,1,0:T(2,128)(2,1)S(1)}, u32[]{:S(2)}, u32[]{:S(2)}) collective-permute-start(bf16[18,1,256]{2,1,0:T(2,128)(2,1)S(1)} %get-tuple-element.38), channel_id=1, source_target_pairs={{0,1},{1,2},{2,3},{3,4},{4,5},{5,6},{6,7},{7,8},{8,9},{9,10},{10,1... | collective-permute-start | bytes 27656 | tf_op jit(solution)/shard_map/ppermute | solution.py:14
  84.1 10.8 %collective-permute-start.13 = (bf16[16,32,256]{2,1,0:T(8,128)(2,1)S(1)}, bf16[16,32,256]{2,1,0:T(8,128)(2,1)S(1)}, u32[]{:S(2)}, u32[]{:S(2)}) collective-permute-start(bf16[16,32,256]{2,1,0:T(8,128)(2,1)S(1)} %bitcast.329), channel_id=1, source_target_pairs={{0,256},{256,0},{1,257},{257,1},{2,258},{258,2},{3,259},{259,3},{4... | collective-permute-start | bytes 786440 | tf_op jit(solution)/shard_map/ppermute | solution.py:27
  89.0 7.1 %copy-start.3 = (f32[9,256,256]{2,1,0:T(8,128)}, f32[9,256,256]{2,1,0:T(8,128)S(1)}, u32[]{:S(2)}) copy-start(f32[9,256,256]{2,1,0:T(8,128)S(1)} %fusion.6) | copy-start | bytes 7077892
  99.3 0.9 copy-start.4
  591.3 2.0 copy-start.6
Sparse Core Ops, SparseCore 0:
  100.3 490.8 all-reduce.2
where the time goes:
time: 606 us; the launch traced here: 604 us
  waiting for transfers between devices  515 us (85%)
  starting transfers between devices  45.8 us (8%)
  matrix products  14.9 us (2%)
  between operations  14.7 us (2%)
  local copies, waits for them, and re-layouts  8.72 us (1%)
    psum x1, waiting for transfers between devices, per_device(): lax.psum((grad_first, grad_projection, grad_second), ('section', 'gy', 'g...  491 us
    ppermute x6, starting transfers between devices, padded_2(): before = lax.ppermute(last, axis, up)  23.5 us
    ppermute x6, starting transfers between devices, padded_2(): after = lax.ppermute(initial, axis, down)  13.4 us
    ppermute x2, waiting for transfers between devices, from_partner(): return lax.ppermute(block, axis, route)  12.5 us
  transfers between devices with their start and end apart: 15, of which 9 were waited for; matrix products, arithmetic and copies ran while one was open for 1% of the time, Pallas kernels for 0%

commit v1 on v0

--- a/solution.py
+++ b/solution.py
@@ -1,7 +1,199 @@
+import functools
+
 import jax
 import jax.numpy as jnp
 from jax import lax
+from jax.experimental import pallas as pl
+from jax.experimental.pallas import tpu as pltpu
 from jax.sharding import PartitionSpec as P
+
+
+MESH = pl.DeviceIdType.MESH
+F32, BF16 = jnp.float32, jnp.bfloat16
+UNITS = 12
+def coords():
+    s, g, z = lax.axis_index("section"), lax.axis_index("gy"), lax.axis_index("gx")
+    core = lax.rem(g, 2)
+    x = s * 2 + lax.rem(lax.div(g, 2), 2)
+    y = lax.div(g, 4)
+    return x, y, core, z
+
+def dev(x, y, core, z):
+    return (lax.div(x, 2), y * 4 + lax.rem(x, 2) * 2 + core, z)
+
+def ar_kernel(chunks, stop, a_ref, out, r0, h0, r1, h1, r2, h2, zb, *sems):
+    (s0s, s0r, s1s, s1r, s2s, s2r, zs, zr, gzs, gzr, g2s, g2r, g1s, g1r, g0s, g0r) = sems
+    x, y, core, z = coords()
+    mod4 = lambda v: lax.rem(v, 4)
+    sib = dev(x, y, 1 - core, z)
+    barrier = pltpu.get_barrier_semaphore()
+    pl.semaphore_signal(barrier, inc=1, device_id=sib, device_id_type=MESH)
+    for d in range(1, 4):
+        pl.semaphore_signal(barrier, inc=1, device_id=dev(mod4(x + d), y, core, z), device_id_type=MESH)
+        pl.semaphore_signal(barrier, inc=1, device_id=dev(x, mod4(y + d), core, z), device_id_type=MESH)
+    for d in range(1, 16):
+        pl.semaphore_signal(barrier, inc=1, device_id=dev(x, y, core, lax.rem(z + d, 16)), device_id_type=MESH)
+    pl.semaphore_wait(barrier, 22)
+
+    mine = pl.ds(pl.multiple_of(core * 128, 128), 128)
+    other = pl.ds(pl.multiple_of((1 - core) * 128, 128), 128)
+    sends = []
+
+    def push(src, dst, ss, rs, to):
+        c = pltpu.make_async_remote_copy(src_ref=src, dst_ref=dst, send_sem=ss, recv_sem=rs, device_id=to, device_id_type=MESH)
+        c.start()
+        sends.append(c)
+        return c
+
+    def axes(yfirst):
+        if yfirst:
+            return (y, lambda p: dev(x, p, core, z)), (x, lambda p: dev(p, y, core, z))
+        return (x, lambda p: dev(p, y, core, z)), (y, lambda p: dev(x, p, core, z))
+
+    def st0(ci, ch):
+        u0, n, yf = ch
+        us = pl.ds(u0, n)
+        return [push(a_ref.at[us, :, other], r0.at[us], s0s.at[ci], s0r.at[ci], sib)]
+
+    def st1(ci, ch, c):
+        u0, n, yf = ch
+        us = pl.ds(u0, n)
+        c[0].wait_recv()
+        h0[us] = (a_ref[us, :, mine].astype(F32) + r0[us].astype(F32)).astype(BF16)
+        (fm, fd), _ = axes(yf)
+        out_c = []
+        for d in range(1, 4):
+            p = mod4(fm + d)
+            out_c.append(push(h0.at[us, pl.ds(pl.multiple_of(p * 64, 64), 64)], r1.at[d - 1, us], s1s.at[ci, d - 1], s1r.at[ci, d - 1], fd(p)))
+        return out_c
+
+    def st2(ci, ch, c):
+        u0, n, yf = ch
+        us = pl.ds(u0, n)
+        for k in c:
+            k.wait_recv()
+        (fm, fd), (sm, sd) = axes(yf)
+        h1[us] = (h0[us, pl.ds(pl.multiple_of(fm * 64, 64), 64)].astype(F32) + r1[0, us].astype(F32) + r1[1, us].astype(F32) + r1[2, us].astype(F32)).astype(BF16)
+        out_c = []
+        for d in range(1, 4):
+            p = mod4(sm + d)
+            out_c.append(push(h1.at[us, pl.ds(pl.multiple_of(p * 16, 16), 16)], r2.at[d - 1, us], s2s.at[ci, d - 1], s2r.at[ci, d - 1], sd(p)))
+        return out_c
+
+    def st3(ci, ch, c):
+        u0, n, yf = ch
+        us = pl.ds(u0, n)
+        for k in c:
+            k.wait_recv()
+        (fm, fd), (sm, sd) = axes(yf)
+        h2[us] = (h1[us, pl.ds(pl.multiple_of(sm * 16, 16), 16)].astype(F32) + r2[0, us].astype(F32) + r2[1, us].astype(F32) + r2[2, us].astype(F32)).astype(BF16)
+        for u in range(u0, u0 + n):
+            @pl.when(z != u)
+            def _():
+                pltpu.make_async_remote_copy(src_ref=h2.at[u], dst_ref=zb.at[z], send_sem=zs.at[u], recv_sem=zr, device_id=dev(x, y, core, u), device_id_type=MESH).start()
+        return None
+
+    def rows16(yf):
+        (fm, fd), (sm, sd) = axes(yf)
+        return pl.ds(pl.multiple_of(fm * 64 + sm * 16, 16), 16)
+
+    def rows64(yf):
+        (fm, fd), (sm, sd) = axes(yf)
+        return pl.ds(pl.multiple_of(fm * 64, 64), 64)
+
+    def st4(ci, ch, c):
+        u0, n, yf = ch
+        r16 = rows16(yf)
+        @pl.when(jnp.logical_and(z >= u0, z < u0 + n))
+        def _():
+            zb[z] = h2[z]
+            pltpu.make_async_copy(zb.at[pl.ds(0, 15)], zb.at[pl.ds(0, 15)], zr).wait()
+            tot = zb[0].astype(F32)
+            for k in range(1, 16):
+                tot = tot + zb[k].astype(F32)
+            out[z, r16, mine] = tot.astype(BF16)
+            for d in range(1, 16):
+                to = lax.rem(z + d, 16)
+                pltpu.make_async_remote_copy(src_ref=out.at[z, r16, mine], dst_ref=out.at[z, r16, mine], send_sem=gzs, recv_sem=gzr.at[z], device_id=dev(x, y, core, to), device_id_type=MESH).start()
+        return None
+
+    def st5(ci, ch, c):
+        u0, n, yf = ch
+        us = pl.ds(u0, n)
+        r16 = rows16(yf)
+        for u in range(u0, u0 + n):
+            @pl.when(z != u)
+            def _():
+                pltpu.make_async_copy(out.at[u, r16, mine], out.at[u, r16, mine], gzr.at[u]).wait()
+        (fm, fd), (sm, sd) = axes(yf)
+        return [push(out.at[us, r16, mine], out.at[us, r16, mine], g2s.at[ci, d - 1], g2r.at[ci, d - 1], sd(mod4(sm + d))) for d in range(1, 4)]
+
+    def st6(ci, ch, c):
+        u0, n, yf = ch
+        us = pl.ds(u0, n)
+        for k in c:
+            k.wait_recv()
+        r64 = rows64(yf)
+        (fm, fd), (sm, sd) = axes(yf)
+        return [push(out.at[us, r64, mine], out.at[us, r64, mine], g1s.at[ci, d - 1], g1r.at[ci, d - 1], fd(mod4(fm + d))) for d in range(1, 4)]
+
+    def st7(ci, ch, c):
+        u0, n, yf = ch
+        us = pl.ds(u0, n)
+        for k in c:
+            k.wait_recv()
+        return [push(out.at[us, :, mine], out.at[us, :, mine], g0s.at[ci], g0r.at[ci], sib)]
+
+    if stop == 0:
+        return
+    state = [st0(ci, ch) for ci, ch in enumerate(chunks)]
+    for k, st in enumerate((st1, st2, st3, st4, st5, st6, st7)):
+        if k + 2 > stop:
+            break
+        state = [st(ci, ch, state[ci]) for ci, ch in enumerate(chunks)]
+    for c in state:
+        for e in c or []:
+            e.wait_recv()
+    for c in sends:
+        c.wait_send()
+    if stop >= 4:
+        for u in range(UNITS):
+            @pl.when(z != u)
+            def _():
+                pltpu.make_async_copy(h2.at[u], h2.at[u], zs.at[u]).wait()
+    if stop == 4:
+        @pl.when(z < UNITS)
+        def _():
+            pltpu.make_async_copy(zb.at[pl.ds(0, 15)], zb.at[pl.ds(0, 15)], zr).wait()
+    if stop == 5:
+        for u in range(UNITS):
+            @pl.when(z != u)
+            def _():
+                pltpu.make_async_copy(h2.at[u], h2.at[u], gzr.at[u]).wait()
+    if stop >= 5:
+        @pl.when(z < UNITS)
+        def _():
+            pltpu.make_async_copy(zb.at[pl.ds(0, 15)], zb.at[pl.ds(0, 15)], gzs).wait()
+
+def ar(a, chunks, cid=0, stop=8):
+    n = len(chunks)
+    D = pltpu.SemaphoreType.DMA
+    return pl.pallas_call(
+        functools.partial(ar_kernel, chunks, stop),
+        out_shape=jax.ShapeDtypeStruct((UNITS, 256, 256), BF16),
+        in_specs=[pl.BlockSpec(memory_space=pltpu.VMEM)],
+        out_specs=pl.BlockSpec(memory_space=pltpu.VMEM),
+        scratch_shapes=[
+            pltpu.VMEM((UNITS, 256, 128), BF16), pltpu.VMEM((UNITS, 256, 128), BF16),
+            pltpu.VMEM((3, UNITS, 64, 128), BF16), pltpu.VMEM((UNITS, 64, 128), BF16),
+            pltpu.VMEM((3, UNITS, 16, 128), BF16), pltpu.VMEM((UNITS, 16, 128), BF16),
+            pltpu.VMEM((16, 16, 128), BF16),
+            D((n,)), D((n,)), D((n, 3)), D((n, 3)), D((n, 3)), D((n, 3)),
+            D((UNITS,)), D(()), D(()), D((UNITS,)),
+            D((n, 3)), D((n, 3)), D((n, 3)), D((n, 3)), D((n,)), D((n,)),
+        ],
+        compiler_params=pltpu.CompilerParams(collective_id=cid, has_side_effects=True, vmem_limit_bytes=40 << 20),
+    )(a)
 
 
 def padded_2(array, sides, width):
@@ -135,9 +327,22 @@
     back = from_partner(back_far, "section", 0)
     grad_projection, pooled_slope = projection_back(pooled, back, projection)
     grad_first = first_back(padded, before, pooled_slope)
-    grad_first, grad_projection, grad_second = lax.psum(
-        (grad_first, grad_projection, grad_second), ("section", "gy", "gx")
-    )
+    blocks = jnp.concatenate(
+        [
+            grad_first.reshape(9, 128, 128),
+            jnp.zeros((1, 128, 128), jnp.float32),
+            grad_projection[None, :, :128],
+            grad_projection[None, :, 128:],
+        ]
+    )
+    small = blocks.reshape(3, 2, 2, 128, 128).transpose(0, 1, 3, 2, 4).reshape(3, 256, 256)
+    packed = jnp.concatenate([grad_second.reshape(9, 256, 256), small]).astype(jnp.bfloat16)
+    total = ar(packed, ((0, 6, True), (6, 6, False)))
+    grad_second = total[:9].reshape(3, 3, 256, 256).astype(jnp.float32)
+    blocks = total[9:].reshape(3, 2, 128, 2, 128).transpose(0, 1, 3, 2, 4).reshape(12, 128, 128)
+    blocks = blocks.astype(jnp.float32)
+    grad_first = blocks[:9].reshape(3, 3, 128, 128)
+    grad_projection = jnp.concatenate([blocks[10], blocks[11]], axis=1)
     return (output[None], grad_first, grad_projection, grad_second)
 
 

time: 606 us -> 158 us (0.26)
  waiting for transfers between devices: 515 us -> 24.1 us
  Pallas kernels: 0 us -> 58.4 us
  between operations: 14.7 us -> 1.32 us
    psum x1 -> x0, waiting for transfers between devices: 491 us -> none  [per_device(): lax.psum((grad_first, grad_projection, grad_second), ('section', 'gy', 'g...]
    pallas_call x0 -> x1, Pallas kernels: none -> 58.4 us  [ar(): pl.pallas_call(functools.partial(ar_kernel, chunks, stop), out_shape=jax....]
  transfers between devices with their start and end apart: 15 -> 14, of which waited for: 9 -> 8; matrix products, arithmetic and copies ran while one was open for 1% -> 3% of each run, Pallas kernels for 0% -> 0%
where the time goes in v1:
time: 158 us; the launch traced here: 157 us
  Pallas kernels  58.4 us (37%)
  starting transfers between devices  45.7 us (29%)
  waiting for transfers between devices  24.1 us (15%)
  matrix products  14.4 us (9%)
  other arithmetic  7 us (4%)
  local copies, waits for them, and re-layouts  6.48 us (4%)
    pallas_call x1, Pallas kernels, ar(): pl.pallas_call(functools.partial(ar_kernel, chunks, stop), out_shape=jax....  58.4 us
    ppermute x6, starting transfers between devices, padded_2(): before = lax.ppermute(last, axis, up)  23.5 us
    ppermute x6, starting transfers between devices, padded_2(): after = lax.ppermute(initial, axis, down)  13.4 us
    ppermute x2, waiting for transfers between devices, from_partner(): return lax.ppermute(block, axis, route)  12.4 us
    ppermute x6, waiting for transfers between devices, padded_2(): after = lax.ppermute(initial, axis, down)  11.1 us
    ppermute x2, starting transfers between devices, from_partner(): return lax.ppermute(block, axis, route)  8.8 us
    dot_general x18, matrix products, conv_slopes(): jnp.einsum('pc,pd->cd', piece, slope, preferred_element_type=jnp.float32)  5.76 us
    dot_general x18, matrix products, conv_forward(): jnp.dot(piece, kernel[row_tap, col_tap], preferred_element_type=jnp.float32)  5.65 us
  transfers between devices with their start and end apart: 14, of which 8 were waited for; matrix products, arithmetic and copies ran while one was open for 3% of the time, Pallas kernels for 0%

profile of v1, /device:TPU:1, one launch (start us, length us, event | category | flops | bytes accessed | tf_op | source)
XLA Modules:
  0.0 157.4 jit_solution(10708399172545005772)
XLA Ops:
  0.7 0.8 slice_bitcast_fusion.7
  1.4 4.5 %collective-permute-start = (bf16[1,64,128]{2,1,0:T(8,128)(2,1)S(1)}, bf16[1,64,128]{2,1,0:T(8,128)(2,1)S(1)}, u32[]{:S(2)}, u32[]{:S(2)}) collective-permute-start(bf16[1,64,128]{2,1,0:T(8,128)(2,1)S(1)} %get-tuple-element.20), channel_id=1, source_target_pairs={{0,16},{16,32},{32,48},{48,64},{64,80},{80,96},{96,112},{112,128},... | collective-permute-start | bytes 49160 | tf_op jit(solution)/shard_map/ppermute | solution.py:206
  5.9 5.6 %collective-permute-start.1 = (bf16[1,64,128]{2,1,0:T(8,128)(2,1)S(1)}, bf16[1,64,128]{2,1,0:T(8,128)(2,1)S(1)}, u32[]{:S(2)}, u32[]{:S(2)}) collective-permute-start(bf16[1,64,128]{2,1,0:T(8,128)(2,1)S(1)} %get-tuple-element.21), channel_id=1, source_target_pairs={{16,0},{32,16},{48,32},{64,48},{80,64},{96,80},{112,96},{128,112},... | collective-permute-start | bytes 49160 | tf_op jit(solution)/shard_map/ppermute | solution.py:207
  11.5 0.8 collective-permute-done.1
  12.3 0.9 pad_maximum_fusion.16
  13.2 2.2 %collective-permute-start.2 = (bf16[34,1,128]{2,1,0:T(2,128)(2,1)S(1)}, bf16[34,1,128]{2,1,0:T(2,128)(2,1)S(1)}, u32[]{:S(2)}, u32[]{:S(2)}) collective-permute-start(bf16[34,1,128]{2,1,0:T(2,128)(2,1)S(1)} %get-tuple-element.14), channel_id=1, source_target_pairs={{0,1},{1,2},{2,3},{3,4},{4,5},{5,6},{6,7},{7,8},{8,9},{9,10},{10,1... | collective-permute-start | bytes 26120 | tf_op jit(solution)/shard_map/ppermute | solution.py:206
  15.5 1.4 collective-permute-start.3
  16.9 1.4 pad_maximum_fusion.1
  18.3 0.3 fusion.100
  18.6 1.7 %collective-permute-done.3 = bf16[34,1,128]{2,1,0:T(2,128)(2,1)S(1)} collective-permute-done((bf16[34,1,128]{2,1,0:T(2,128)(2,1)S(1)}, bf16[34,1,128]{2,1,0:T(2,128)(2,1)S(1)}, u32[]{:S(2)}, u32[]{:S(2)}) %collective-permute-start.3) | collective-permute-done | bytes 8736 | tf_op jit(solution)/shard_map/ppermute | solution.py:207
  20.3 0.3 maximum_maximum_fusion
  20.6 0.6 fusion.112
  21.2 0.3 fusion.92
  21.5 0.3 convolution_add_fusion.6
  21.8 0.3 convolution_add_fusion.5
  22.1 0.3 convolution_add_fusion.4
  22.4 0.3 convolution_add_fusion.3
  22.7 0.3 convolution_add_fusion.2
  23.0 0.3 convolution_add_fusion.1
  23.3 0.5 multiply_convert_fusion.1
  23.7 0.8 convert_reduce_fusion
  24.9 4.5 %collective-permute-start.4 = (bf16[16,32,256]{2,1,0:T(8,128)(2,1)S(1)}, bf16[16,32,256]{2,1,0:T(8,128)(2,1)S(1)}, u32[]{:S(2)}, u32[]{:S(2)}) collective-permute-start(bf16[16,32,256]{2,1,0:T(8,128)(2,1)S(1)} %bitcast.352), channel_id=1, source_target_pairs={{0,256},{256,0},{1,257},{257,1},{2,258},{258,2},{3,259},{259,3},{4... | collective-permute-start | bytes 786440 | tf_op jit(solution)/shard_map/ppermute | solution.py:219
  29.3 6.6 %collective-permute-done.4 = bf16[16,32,256]{2,1,0:T(8,128)(2,1)S(1)} collective-permute-done((bf16[16,32,256]{2,1,0:T(8,128)(2,1)S(1)}, bf16[16,32,256]{2,1,0:T(8,128)(2,1)S(1)}, u32[]{:S(2)}, u32[]{:S(2)}) %collective-permute-start.4) | collective-permute-done | bytes 262176 | tf_op jit(solution)/shard_map/ppermute | solution.py:219
  35.9 4.5 %collective-permute-start.5 = (bf16[1,32,256]{2,1,0:T(8,128)(2,1)S(1)}, bf16[1,32,256]{2,1,0:T(8,128)(2,1)S(1)}, u32[]{:S(2)}, u32[]{:S(2)}) collective-permute-start(bf16[1,32,256]{2,1,0:T(8,128)(2,1)S(1)} %get-tuple-element.51), channel_id=1, source_target_pairs={{0,16},{16,32},{32,48},{48,64},{64,80},{80,96},{96,112},{112,128},... | collective-permute-start | bytes 49160 | tf_op jit(solution)/shard_map/ppermute | solution.py:206
  40.4 1.9 %collective-permute-start.6 = (bf16[1,32,256]{2,1,0:T(8,128)(2,1)S(1)}, bf16[1,32,256]{2,1,0:T(8,128)(2,1)S(1)}, u32[]{:S(2)}, u32[]{:S(2)}) collective-permute-start(bf16[1,32,256]{2,1,0:T(8,128)(2,1)S(1)} %get-tuple-element.50), channel_id=1, source_target_pairs={{16,0},{32,16},{48,32},{64,48},{80,64},{96,80},{112,96},{128,112},... | collective-permute-start | bytes 49160 | tf_op jit(solution)/shard_map/ppermute | solution.py:207
  42.3 3.1 %collective-permute-done.6 = bf16[1,32,256]{2,1,0:T(8,128)(2,1)S(1)} collective-permute-done((bf16[1,32,256]{2,1,0:T(8,128)(2,1)S(1)}, bf16[1,32,256]{2,1,0:T(8,128)(2,1)S(1)}, u32[]{:S(2)}, u32[]{:S(2)}) %collective-permute-start.6) | collective-permute-done | bytes 16416 | tf_op jit(solution)/shard_map/ppermute | solution.py:207
  45.6 3.6 %collective-permute-start.7 = (bf16[18,1,256]{2,1,0:T(2,128)(2,1)S(1)}, bf16[18,1,256]{2,1,0:T(2,128)(2,1)S(1)}, u32[]{:S(2)}, u32[]{:S(2)}) collective-permute-start(bf16[18,1,256]{2,1,0:T(2,128)(2,1)S(1)} %get-tuple-element.41), channel_id=1, source_target_pairs={{0,1},{1,2},{2,3},{3,4},{4,5},{5,6},{6,7},{7,8},{8,9},{9,10},{10,1... | collective-permute-start | bytes 27656 | tf_op jit(solution)/shard_map/ppermute | solution.py:206
  49.2 1.3 collective-permute-start.8
  50.9 4.1 %collective-permute-done.8 = bf16[18,1,256]{2,1,0:T(2,128)(2,1)S(1)} collective-permute-done((bf16[18,1,256]{2,1,0:T(2,128)(2,1)S(1)}, bf16[18,1,256]{2,1,0:T(2,128)(2,1)S(1)}, u32[]{:S(2)}, u32[]{:S(2)}) %collective-permute-start.8) | collective-permute-done | bytes 9248 | tf_op jit(solution)/shard_map/ppermute | solution.py:207
  55.0 0.4 pad_maximum_fusion.8
  56.8 0.7 copy-done.5
  57.5 1.1 fusion.45
  58.9 3.1 %collective-permute-start.9 = (bf16[1,32,256]{2,1,0:T(8,128)(2,1)S(1)}, bf16[1,32,256]{2,1,0:T(8,128)(2,1)S(1)}, u32[]{:S(2)}, u32[]{:S(2)}) collective-permute-start(bf16[1,32,256]{2,1,0:T(8,128)(2,1)S(1)} %get-tuple-element.45), channel_id=1, source_target_pairs={{0,16},{16,32},{32,48},{48,64},{64,80},{80,96},{96,112},{112,128},... | collective-permute-start | bytes 49160 | tf_op jit(solution)/shard_map/ppermute | solution.py:206
  62.0 1.9 %collective-permute-start.10 = (bf16[1,32,256]{2,1,0:T(8,128)(2,1)S(1)}, bf16[1,32,256]{2,1,0:T(8,128)(2,1)S(1)}, u32[]{:S(2)}, u32[]{:S(2)}) collective-permute-start(bf16[1,32,256]{2,1,0:T(8,128)(2,1)S(1)} %get-tuple-element.46), channel_id=1, source_target_pairs={{16,0},{32,16},{48,32},{64,48},{80,64},{96,80},{112,96},{128,112},... | collective-permute-start | bytes 49160 | tf_op jit(solution)/shard_map/ppermute | solution.py:207
  64.5 0.3 fusion.15
  64.8 0.3 fusion.17
  65.1 0.3 fusion.19
  65.3 0.3 fusion.21
  65.6 1.4 collective-permute-done.10
  67.1 1.3 collective-permute-start.11
  68.4 5.6 %collective-permute-start.12 = (bf16[18,1,256]{2,1,0:T(2,128)(2,1)S(1)}, bf16[18,1,256]{2,1,0:T(2,128)(2,1)S(1)}, u32[]{:S(2)}, u32[]{:S(2)}) collective-permute-start(bf16[18,1,256]{2,1,0:T(2,128)(2,1)S(1)} %get-tuple-element.37), channel_id=1, source_target_pairs={{0,1},{1,2},{2,3},{3,4},{4,5},{5,6},{6,7},{7,8},{8,9},{9,10},{10,1... | collective-permute-start | bytes 27656 | tf_op jit(solution)/shard_map/ppermute | solution.py:206
  74.4 0.6 collective-permute-done.12
  77.5 4.3 %collective-permute-start.13 = (bf16[16,32,256]{2,1,0:T(8,128)(2,1)S(1)}, bf16[16,32,256]{2,1,0:T(8,128)(2,1)S(1)}, u32[]{:S(2)}, u32[]{:S(2)}) collective-permute-start(bf16[16,32,256]{2,1,0:T(8,128)(2,1)S(1)} %bitcast.353), channel_id=1, source_target_pairs={{0,256},{256,0},{1,257},{257,1},{2,258},{258,2},{3,259},{259,3},{4... | collective-permute-start | bytes 786440 | tf_op jit(solution)/shard_map/ppermute | solution.py:219
  81.8 0.3 fusion.23
  82.4 5.9 %collective-permute-done.13 = bf16[16,32,256]{2,1,0:T(8,128)(2,1)S(1)} collective-permute-done((bf16[16,32,256]{2,1,0:T(8,128)(2,1)S(1)}, bf16[16,32,256]{2,1,0:T(8,128)(2,1)S(1)}, u32[]{:S(2)}, u32[]{:S(2)}) %collective-permute-start.13) | collective-permute-done | bytes 262176 | tf_op jit(solution)/shard_map/ppermute | solution.py:219
  88.5 0.5 broadcast_in_dim.17
  88.9 0.4 multiply_convert_fusion
  89.3 0.4 fusion.28
  89.7 0.4 fusion.30
  90.1 0.4 fusion.32
  90.4 0.4 fusion.34
  90.8 0.4 fusion.36
  91.2 0.4 fusion.38
  91.5 0.4 fusion.40
  91.9 0.4 fusion.42
  92.3 0.4 fusion.44
  92.9 0.4 copy.14
  93.7 58.4 %shard_map.84 = bf16[12,256,256]{2,1,0:T(8,128)(2,1)S(1)} custom-call(bf16[12,256,256]{2,1,0:T(8,128)(2,1)S(1)} %constant_dynamic-update-slice_fusion.6.a_ref), custom_call_target="tpu_custom_call" | custom-call | tf_op jit(solution)/shard_map/pallas_call | solution.py:181
  152.1 1.1 copy-done.1
  153.2 0.4 reshape.199
  153.7 0.9 slice.339
  154.6 0.5 slice-done
  155.1 1.6 %convert.114 = f32[3,3,256,256]{3,2,1,0:T(8,128)} convert(bf16[3,3,256,256]{3,2,1,0:T(8,128)(2,1)S(1)} %bitcast.292) | non-fusion elementwise | flops 589824 | bytes 3538944 | tf_op jit(solution)/shard_map/convert_element_type | solution.py:341
  156.7 0.7 pad_maximum_fusion.10
  (61 shorter events, 7.0 us)
Async XLA Ops:
  0.6 24.0 %copy-start = (bf16[128,256]{1,0:T(8,128)(2,1)S(1)}, bf16[128,256]{1,0:T(8,128)(2,1)}, u32[]{:S(2)}) copy-start(bf16[128,256]{1,0:T(8,128)(2,1)} %param.7) | copy-start | bytes 196612
  0.6 17.7 %copy-start.4 = (bf16[3,3,128,128]{3,2,1,0:T(8,128)(2,1)S(1)}, bf16[3,3,128,128]{3,2,1,0:T(8,128)(2,1)}, u32[]{:S(2)}) copy-start(bf16[3,3,128,128]{3,2,1,0:T(8,128)(2,1)} %param.6) | copy-start | bytes 884740
  1.4 10.1 %collective-permute-start = (bf16[1,64,128]{2,1,0:T(8,128)(2,1)S(1)}, bf16[1,64,128]{2,1,0:T(8,128)(2,1)S(1)}, u32[]{:S(2)}, u32[]{:S(2)}) collective-permute-start(bf16[1,64,128]{2,1,0:T(8,128)(2,1)S(1)} %get-tuple-element.20), channel_id=1, source_target_pairs={{0,16},{16,32},{32,48},{48,64},{64,80},{80,96},{96,112},{112,128},... | collective-permute-start | bytes 49160 | tf_op jit(solution)/shard_map/ppermute | solution.py:206
  5.9 6.4 %collective-permute-start.1 = (bf16[1,64,128]{2,1,0:T(8,128)(2,1)S(1)}, bf16[1,64,128]{2,1,0:T(8,128)(2,1)S(1)}, u32[]{:S(2)}, u32[]{:S(2)}) collective-permute-start(bf16[1,64,128]{2,1,0:T(8,128)(2,1)S(1)} %get-tuple-element.21), channel_id=1, source_target_pairs={{16,0},{32,16},{48,32},{64,48},{80,64},{96,80},{112,96},{128,112},... | collective-permute-start | bytes 49160 | tf_op jit(solution)/shard_map/ppermute | solution.py:207
  13.2 5.4 %collective-permute-start.2 = (bf16[34,1,128]{2,1,0:T(2,128)(2,1)S(1)}, bf16[34,1,128]{2,1,0:T(2,128)(2,1)S(1)}, u32[]{:S(2)}, u32[]{:S(2)}) collective-permute-start(bf16[34,1,128]{2,1,0:T(2,128)(2,1)S(1)} %get-tuple-element.14), channel_id=1, source_target_pairs={{0,1},{1,2},{2,3},{3,4},{4,5},{5,6},{6,7},{7,8},{8,9},{9,10},{10,1... | collective-permute-start | bytes 26120 | tf_op jit(solution)/shard_map/ppermute | solution.py:206
  15.5 4.8 %copy-start.2 = (bf16[1,32,64,128]{3,2,1,0:T(8,128)(2,1)S(1)}, bf16[1,32,64,128]{3,2,1,0:T(8,128)(2,1)}, u32[]{:S(2)}) copy-start(bf16[1,32,64,128]{3,2,1,0:T(8,128)(2,1)} %param.5) | copy-start | bytes 1572868
  15.5 4.8 %collective-permute-start.3 = (bf16[34,1,128]{2,1,0:T(2,128)(2,1)S(1)}, bf16[34,1,128]{2,1,0:T(2,128)(2,1)S(1)}, u32[]{:S(2)}, u32[]{:S(2)}) collective-permute-start(bf16[34,1,128]{2,1,0:T(2,128)(2,1)S(1)} %get-tuple-element.15), channel_id=1, source_target_pairs={{1,0},{2,1},{3,2},{4,3},{5,4},{6,5},{7,6},{8,7},{9,8},{10,9},{11,1... | collective-permute-start | bytes 26120 | tf_op jit(solution)/shard_map/ppermute | solution.py:207
  24.6 25.9 %copy-start.3 = (bf16[3,3,256,256]{3,2,1,0:T(8,128)(2,1)S(1)}, bf16[3,3,256,256]{3,2,1,0:T(8,128)(2,1)}, u32[]{:S(2)}) copy-start(bf16[3,3,256,256]{3,2,1,0:T(8,128)(2,1)} %param.8) | copy-start | bytes 3538948
  24.9 11.0 %collective-permute-start.4 = (bf16[16,32,256]{2,1,0:T(8,128)(2,1)S(1)}, bf16[16,32,256]{2,1,0:T(8,128)(2,1)S(1)}, u32[]{:S(2)}, u32[]{:S(2)}) collective-permute-start(bf16[16,32,256]{2,1,0:T(8,128)(2,1)S(1)} %bitcast.352), channel_id=1, source_target_pairs={{0,256},{256,0},{1,257},{257,1},{2,258},{258,2},{3,259},{259,3},{4... | collective-permute-start | bytes 786440 | tf_op jit(solution)/shard_map/ppermute | solution.py:219
  35.9 6.4 %collective-permute-start.5 = (bf16[1,32,256]{2,1,0:T(8,128)(2,1)S(1)}, bf16[1,32,256]{2,1,0:T(8,128)(2,1)S(1)}, u32[]{:S(2)}, u32[]{:S(2)}) collective-permute-start(bf16[1,32,256]{2,1,0:T(8,128)(2,1)S(1)} %get-tuple-element.51), channel_id=1, source_target_pairs={{0,16},{16,32},{32,48},{48,64},{64,80},{80,96},{96,112},{112,128},... | collective-permute-start | bytes 49160 | tf_op jit(solution)/shard_map/ppermute | solution.py:206
  40.4 5.1 %collective-permute-start.6 = (bf16[1,32,256]{2,1,0:T(8,128)(2,1)S(1)}, bf16[1,32,256]{2,1,0:T(8,128)(2,1)S(1)}, u32[]{:S(2)}, u32[]{:S(2)}) collective-permute-start(bf16[1,32,256]{2,1,0:T(8,128)(2,1)S(1)} %get-tuple-element.50), channel_id=1, source_target_pairs={{16,0},{32,16},{48,32},{64,48},{80,64},{96,80},{112,96},{128,112},... | collective-permute-start | bytes 49160 | tf_op jit(solution)/shard_map/ppermute | solution.py:207
  45.6 5.3 %collective-permute-start.7 = (bf16[18,1,256]{2,1,0:T(2,128)(2,1)S(1)}, bf16[18,1,256]{2,1,0:T(2,128)(2,1)S(1)}, u32[]{:S(2)}, u32[]{:S(2)}) collective-permute-start(bf16[18,1,256]{2,1,0:T(2,128)(2,1)S(1)} %get-tuple-element.41), channel_id=1, source_target_pairs={{0,1},{1,2},{2,3},{3,4},{4,5},{5,6},{6,7},{7,8},{8,9},{9,10},{10,1... | collective-permute-start | bytes 27656 | tf_op jit(solution)/shard_map/ppermute | solution.py:206
  49.2 5.8 %collective-permute-start.8 = (bf16[18,1,256]{2,1,0:T(2,128)(2,1)S(1)}, bf16[18,1,256]{2,1,0:T(2,128)(2,1)S(1)}, u32[]{:S(2)}, u32[]{:S(2)}) collective-permute-start(bf16[18,1,256]{2,1,0:T(2,128)(2,1)S(1)} %get-tuple-element.42), channel_id=1, source_target_pairs={{1,0},{2,1},{3,2},{4,3},{5,4},{6,5},{7,6},{8,7},{9,8},{10,9},{11,1... | collective-permute-start | bytes 27656 | tf_op jit(solution)/shard_map/ppermute | solution.py:207
  56.5 1.0 copy-start.5
  58.9 6.7 %collective-permute-start.9 = (bf16[1,32,256]{2,1,0:T(8,128)(2,1)S(1)}, bf16[1,32,256]{2,1,0:T(8,128)(2,1)S(1)}, u32[]{:S(2)}, u32[]{:S(2)}) collective-permute-start(bf16[1,32,256]{2,1,0:T(8,128)(2,1)S(1)} %get-tuple-element.45), channel_id=1, source_target_pairs={{0,16},{16,32},{32,48},{48,64},{64,80},{80,96},{96,112},{112,128},... | collective-permute-start | bytes 49160 | tf_op jit(solution)/shard_map/ppermute | solution.py:206
  62.0 5.1 %collective-permute-start.10 = (bf16[1,32,256]{2,1,0:T(8,128)(2,1)S(1)}, bf16[1,32,256]{2,1,0:T(8,128)(2,1)S(1)}, u32[]{:S(2)}, u32[]{:S(2)}) collective-permute-start(bf16[1,32,256]{2,1,0:T(8,128)(2,1)S(1)} %get-tuple-element.46), channel_id=1, source_target_pairs={{16,0},{32,16},{48,32},{64,48},{80,64},{96,80},{112,96},{128,112},... | collective-permute-start | bytes 49160 | tf_op jit(solution)/shard_map/ppermute | solution.py:207
  67.1 7.2 %collective-permute-start.11 = (bf16[18,1,256]{2,1,0:T(2,128)(2,1)S(1)}, bf16[18,1,256]{2,1,0:T(2,128)(2,1)S(1)}, u32[]{:S(2)}, u32[]{:S(2)}) collective-permute-start(bf16[18,1,256]{2,1,0:T(2,128)(2,1)S(1)} %get-tuple-element.36), channel_id=1, source_target_pairs={{1,0},{2,1},{3,2},{4,3},{5,4},{6,5},{7,6},{8,7},{9,8},{10,9},{11,1... | collective-permute-start | bytes 27656 | tf_op jit(solution)/shard_map/ppermute | solution.py:207
  68.4 6.5 %collective-permute-start.12 = (bf16[18,1,256]{2,1,0:T(2,128)(2,1)S(1)}, bf16[18,1,256]{2,1,0:T(2,128)(2,1)S(1)}, u32[]{:S(2)}, u32[]{:S(2)}) collective-permute-start(bf16[18,1,256]{2,1,0:T(2,128)(2,1)S(1)} %get-tuple-element.37), channel_id=1, source_target_pairs={{0,1},{1,2},{2,3},{3,4},{4,5},{5,6},{6,7},{7,8},{8,9},{9,10},{10,1... | collective-permute-start | bytes 27656 | tf_op jit(solution)/shard_map/ppermute | solution.py:206
  77.5 10.8 %collective-permute-start.13 = (bf16[16,32,256]{2,1,0:T(8,128)(2,1)S(1)}, bf16[16,32,256]{2,1,0:T(8,128)(2,1)S(1)}, u32[]{:S(2)}, u32[]{:S(2)}) collective-permute-start(bf16[16,32,256]{2,1,0:T(8,128)(2,1)S(1)} %bitcast.353), channel_id=1, source_target_pairs={{0,256},{256,0},{1,257},{257,1},{2,258},{258,2},{3,259},{259,3},{4... | collective-permute-start | bytes 786440 | tf_op jit(solution)/shard_map/ppermute | solution.py:219
  152.0 1.1 copy-start.1
  153.6 1.5 slice-start

commit v2 on v1

v2 whole, which is shorter than its diff:
```python
import functools

import jax
import jax.numpy as jnp
from jax import lax
from jax.experimental import pallas as pl
from jax.experimental.pallas import tpu as pltpu
from jax.sharding import PartitionSpec as P

MESH = pl.DeviceIdType.MESH
F32, BF16 = jnp.float32, jnp.bfloat16
UNITS = 12
CHUNKS = ((0, 5, True), (5, 4, False), (9, 1, True), (10, 2, False))
AROUND = ((-1, 0), (1, 0), (0, -1), (0, 1), (-1, -1), (-1, 1), (1, -1), (1, 1))


def coords():
    s, g, z = lax.axis_index("section"), lax.axis_index("gy"), lax.axis_index("gx")
    core = lax.rem(g, 2)
    x = s * 2 + lax.rem(lax.div(g, 2), 2)
    return x, lax.div(g, 4), core, z


def dev(x, y, core, z):
    return (lax.div(x, 2), y * 4 + lax.rem(x, 2) * 2 + core, z)


def mod4(v):
    return lax.rem(v, 4)


def dot(left, right, dims=((1,), (0,))):
    return lax.dot_general(left, right, (dims, ((), ())), preferred_element_type=F32)


def sigmoid(v):
    return 0.5 * jnp.tanh(0.5 * v) + 0.5


def network(
    img, k1, proj, k2, cot, out, feat,
    xf, xs, w1, d1, pool, mf, m3, cotf, sf, si, s3, ms, s1, fb, pack,
    colpack, rows_in, cols_in, corners_in, cotpack, cot_in, cot_rows, cot_cols,
    r0, h0, r1, h1, r2, h2, zb,
    hs, hr, cs, cr, fs, fr,
    s0s, s0r, s1s, s1r, s2s, s2r, zs, zr, gzs, gzr, g2s, g2r, g1s, g1r, g0s, g0r,
):
    x, y, core, z = coords()
    sec, gy = lax.axis_index("section"), lax.axis_index("gy")
    other_sec = 1 - sec
    sib = dev(x, y, 1 - core, z)

    def near(s, dy, dx):
        return (s, lax.rem(gy + dy + 16, 16), lax.rem(z + dx + 16, 16))

    barrier = pltpu.get_barrier_semaphore()

    def greet(to):
        pl.semaphore_signal(barrier, inc=1, device_id=to, device_id_type=MESH)

    for dy, dx in AROUND:
        greet(near(sec, dy, dx))
        greet(near(other_sec, dy, dx))
    greet(near(other_sec, 0, 0))
    greet(sib)
    for d in range(1, 4):
        greet(dev(mod4(x + d), y, core, z))
        greet(dev(x, mod4(y + d), core, z))
    for d in range(1, 16):
        greet(dev(x, y, core, lax.rem(z + d, 16)))

    xf[5:37, 24:88] = img[...].astype(F32)
    colpack[0] = xf[5:37, 24:32].reshape(256, 128).astype(BF16)
    colpack[1] = xf[5:37, 80:88].reshape(256, 128).astype(BF16)
    cotf[0:16, 0:32] = cot[...].astype(F32)
    cotpack[0] = cotf[0:16, 0, :].astype(BF16)
    cotpack[1] = cotf[0:16, 31, :].astype(BF16)

    pl.semaphore_wait(barrier, 39)
    sends = []

    def push(src, dst, ss, rs, to):
        c = pltpu.make_async_remote_copy(
            src_ref=src, dst_ref=dst, send_sem=ss, recv_sem=rs, device_id=to, device_id_type=MESH
        )
        c.start()
        sends.append(c)
        return c

    halo = [
        push(img.at[0:5], rows_in.at[1], hs.at[0], hr.at[0], near(sec, -1, 0)),
        push(img.at[27:32], rows_in.at[0], hs.at[1], hr.at[1], near(sec, 1, 0)),
        push(colpack.at[0], cols_in.at[1], hs.at[2], hr.at[2], near(sec, 0, -1)),
        push(colpack.at[1], cols_in.at[0], hs.at[3], hr.at[3], near(sec, 0, 1)),
        push(colpack.at[0, 0:48], corners_in.at[3], hs.at[4], hr.at[4], near(sec, -1, -1)),
        push(colpack.at[1, 0:48], corners_in.at[2], hs.at[5], hr.at[5], near(sec, -1, 1)),
        push(colpack.at[0, 208:256], corners_in.at[1], hs.at[6], hr.at[6], near(sec, 1, -1)),
        push(colpack.at[1, 208:256], corners_in.at[0], hs.at[7], hr.at[7], near(sec, 1, 1)),
    ]
    cots = [
        push(cot, cot_in, cs.at[0], cr.at[0], near(other_sec, 0, 0)),
        push(cot.at[0], cot_rows.at[1], cs.at[1], cr.at[1], near(other_sec, -1, 0)),
        push(cot.at[15], cot_rows.at[0], cs.at[2], cr.at[2], near(other_sec, 1, 0)),
        push(cotpack.at[0], cot_cols.at[1, 1], cs.at[3], cr.at[3], near(other_sec, 0, -1)),
        push(cotpack.at[1], cot_cols.at[0, 1], cs.at[4], cr.at[4], near(other_sec, 0, 1)),
        push(cotpack.at[0], cot_cols.at[1, 2], cs.at[5], cr.at[5], near(other_sec, -1, -1)),
        push(cotpack.at[1], cot_cols.at[0, 2], cs.at[6], cr.at[6], near(other_sec, -1, 1)),
        push(cotpack.at[0], cot_cols.at[1, 0], cs.at[7], cr.at[7], near(other_sec, 1, -1)),
        push(cotpack.at[1], cot_cols.at[0, 0], cs.at[8], cr.at[8], near(other_sec, 1, 1)),
    ]

    zero = jnp.zeros((128, 128), BF16)
    for a in range(3):
        w1[a, 384:512, 0:128] = zero
        w1[a, 0:128, 128:256] = zero
        for b in range(3):
            w1[a, b * 128 : b * 128 + 128, 0:128] = k1[a, b]
            w1[a, b * 128 + 128 : b * 128 + 256, 128:256] = k1[a, b]
    xf[:, 0:16] = jnp.zeros((42, 16, 128), F32)
    xf[:, 96:112] = jnp.zeros((42, 16, 128), F32)
    mf[:, 0:8] = jnp.zeros((20, 8, 256), F32)
    mf[:, 56:64] = jnp.zeros((20, 8, 256), F32)
    cotf[...] = jnp.zeros((18, 48, 256), F32)

    for c in halo:
        c.wait_recv()
    xf[0:5, 24:88] = rows_in[0].astype(F32)
    xf[37:42, 24:88] = rows_in[1].astype(F32)
    for side, at in ((0, 16), (1, 88)):
        xf[5:37, at : at + 8] = cols_in[side].astype(F32).reshape(32, 8, 128)
        xf[0:5, at : at + 8] = corners_in[side].astype(F32).reshape(6, 8, 128)[1:6]
        xf[37:42, at : at + 8] = corners_in[2 + side].astype(F32).reshape(6, 8, 128)[0:5]

    @pl.when(gy == 0)
    def _():
        xf[0:5, 16:96] = jnp.zeros((5, 80, 128), F32)

    @pl.when(gy == 15)
    def _():
        xf[37:42, 16:96] = jnp.zeros((5, 80, 128), F32)

    @pl.when(z == 0)
    def _():
        xf[:, 16:24] = jnp.zeros((42, 8, 128), F32)

    @pl.when(z == 15)
    def _():
        xf[:, 88:96] = jnp.zeros((42, 8, 128), F32)

    @pl.loop(0, 21)
    def _(t):
        rs = pl.ds(t * 2, 2)
        for p in range(4):
            lanes = slice(p * 128, p * 128 + 128)
            xs[rs, 0:32, lanes] = xf[rs, pl.ds(23 + p, 32, 2), :].astype(BF16)
            right = xf[rs, pl.ds(87 + p, 8, 2), :]
            left = xf[rs, pl.ds(7 + p, 8, 2), :]
            xs[rs, 32:48, lanes] = jnp.concatenate([right, left], axis=1).astype(BF16)

    @pl.loop(0, 5)
    def _(t):
        acc = dot(xs[pl.ds(t * 8, 8)].reshape(384, 512), w1[0])
        acc += dot(xs[pl.ds(t * 8 + 1, 8)].reshape(384, 512), w1[1])
        acc += dot(xs[pl.ds(t * 8 + 2, 8)].reshape(384, 512), w1[2])
        sig = sigmoid(acc)
        hid = (acc * sig).astype(BF16).astype(F32).reshape(4, 2, 48, 256)
        slope = sig * (1.0 + acc * (1.0 - sig))
        d1[pl.ds(t * 8, 8)] = slope.reshape(8, 48, 256)[:, 0:32]
        total = hid[:, 0] + hid[:, 1]
        total = (total[:, :, 0:128] + total[:, :, 128:256]) * 0.25
        row = lax.broadcasted_iota(jnp.int32, (4, 48, 128), 0) + (t * 4 - 2 + gy * 16)
        k = lax.broadcasted_iota(jnp.int32, (4, 48, 128), 1)
        col = jnp.where(k < 40, k, k - 48) + z * 32
        inside = (row >= 0) & (row < 256) & (col >= 0) & (col < 512)
        pooled = jnp.where(inside, total, 0.0).astype(BF16)
        pool[pl.ds(t * 4, 4)] = pooled[:, 0:32]
        mid = dot(pooled.reshape(192, 128), proj[...]).astype(BF16).astype(F32).reshape(4, 48, 256)
        mf[pl.ds(t * 4, 4), 16:56] = mid[:, 0:40]
        mf[pl.ds(t * 4, 4), 8:16] = mid[:, 40:48]

    @pl.loop(0, 10)
    def _(t):
        rs = pl.ds(t * 2, 2)
        for b in range(3):
            lanes = slice(b * 256, b * 256 + 256)
            m3[rs, 0:32, lanes] = mf[rs, 15 + b : 47 + b, :].astype(BF16)
            sides = [mf[rs, 47 + b : 55 + b, :], mf[rs, 7 + b : 15 + b, :]]
            m3[rs, 32:48, lanes] = jnp.concatenate(sides, axis=1).astype(BF16)

    for c in cots:
        c.wait_recv()
    cotf[1:17, 0:32] = cot_in[...].astype(F32)
    cotf[0, 0:32] = cot_rows[0].astype(F32)
    cotf[17, 0:32] = cot_rows[1].astype(F32)
    for side, at in ((0, 47), (1, 32)):
        column = cot_cols[side, 1].astype(F32)
        for q in range(16):
            cotf[1 + q, at : at + 1, :] = column[q : q + 1]
        cotf[0, at : at + 1, :] = cot_cols[side, 0].astype(F32)[15:16]
        cotf[17, at : at + 1, :] = cot_cols[side, 2].astype(F32)[0:1]

    @pl.when(gy == 0)
    def _():
        cotf[0] = jnp.zeros((48, 256), F32)

    @pl.when(gy == 15)
    def _():
        cotf[17] = jnp.zeros((48, 256), F32)

    @pl.when(z == 0)
    def _():
        cotf[:, 40:48] = jnp.zeros((18, 8, 256), F32)

    @pl.when(z == 15)
    def _():
        cotf[:, 32:40] = jnp.zeros((18, 8, 256), F32)

    @pl.loop(0, 3)
    def _(t):
        acc = dot(m3[pl.ds(t * 6, 6)].reshape(288, 768), k2[0].reshape(768, 256))
        acc += dot(m3[pl.ds(t * 6 + 1, 6)].reshape(288, 768), k2[1].reshape(768, 256))
        acc += dot(m3[pl.ds(t * 6 + 2, 6)].reshape(288, 768), k2[2].reshape(768, 256))
        sig = sigmoid(acc)
        fb[pl.ds(t * 6, 6)] = (acc * sig).astype(BF16).reshape(6, 48, 256)[:, 0:32]
        slope = (sig * (1.0 + acc * (1.0 - sig))).reshape(6, 48, 256) * cotf[pl.ds(t * 6, 6)]
        slope = slope.astype(BF16)
        si[pl.ds(t * 6, 6)] = slope[:, 0:32]
        slope = slope.astype(F32)
        sf[pl.ds(t * 6, 6), 16:56] = slope[:, 0:40]
        sf[pl.ds(t * 6, 6), 8:16] = slope[:, 40:48]

    feat_copy = push(fb.at[1:17], feat, fs, fr, near(other_sec, 0, 0))

    for a in range(3):
        grad = dot(m3[a + 1 : a + 17, 0:32].reshape(512, 768), si[1:17].reshape(512, 256), ((0,), (0,)))
        pack[3 * a : 3 * a + 3] = grad.reshape(3, 256, 256).astype(BF16)

    mine = pl.ds(pl.multiple_of(core * 128, 128), 128)
    other = pl.ds(pl.multiple_of((1 - core) * 128, 128), 128)

    def axes(yfirst):
        if yfirst:
            return (y, lambda p: dev(x, p, core, z)), (x, lambda p: dev(p, y, core, z))
        return (x, lambda p: dev(p, y, core, z)), (y, lambda p: dev(x, p, core, z))

    def st0(ci):
        u0, n, yf = CHUNKS[ci]
        us = pl.ds(u0, n)
        return [push(pack.at[us, :, other], r0.at[us], s0s.at[ci], s0r.at[ci], sib)]

    def st1(ci, c):
        u0, n, yf = CHUNKS[ci]
        us = pl.ds(u0, n)
        c[0].wait_recv()
        h0[us] = (pack[us, :, mine].astype(F32) + r0[us].astype(F32)).astype(BF16)
        (fm, fd), _ = axes(yf)
        out_c = []
        for d in range(1, 4):
            p = mod4(fm + d)
            out_c.append(push(h0.at[us, pl.ds(pl.multiple_of(p * 64, 64), 64)], r1.at[d - 1, us], s1s.at[ci, d - 1], s1r.at[ci, d - 1], fd(p)))
        return out_c

    def st2(ci, c):
        u0, n, yf = CHUNKS[ci]
        us = pl.ds(u0, n)
        for k in c:
            k.wait_recv()
        (fm, fd), (sm, sd) = axes(yf)
        h1[us] = (h0[us, pl.ds(pl.multiple_of(fm * 64, 64), 64)].astype(F32) + r1[0, us].astype(F32) + r1[1, us].astype(F32) + r1[2, us].astype(F32)).astype(BF16)
        out_c = []
        for d in range(1, 4):
            p = mod4(sm + d)
            out_c.append(push(h1.at[us, pl.ds(pl.multiple_of(p * 16, 16), 16)], r2.at[d - 1, us], s2s.at[ci, d - 1], s2r.at[ci, d - 1], sd(p)))
        return out_c

    def st3(ci, c):
        u0, n, yf = CHUNKS[ci]
        us = pl.ds(u0, n)
        for k in c:
            k.wait_recv()
        (fm, fd), (sm, sd) = axes(yf)
        h2[us] = (h1[us, pl.ds(pl.multiple_of(sm * 16, 16), 16)].astype(F32) + r2[0, us].astype(F32) + r2[1, us].astype(F32) + r2[2, us].astype(F32)).astype(BF16)
        for u in range(u0, u0 + n):
            @pl.when(z != u)
            def _():
                pltpu.make_async_remote_copy(src_ref=h2.at[u], dst_ref=zb.at[z], send_sem=zs.at[u], recv_sem=zr.at[ci // 2], device_id=dev(x, y, core, u), device_id_type=MESH).start()
        return None

    def rows16(yf):
        (fm, fd), (sm, sd) = axes(yf)
        return pl.ds(pl.multiple_of(fm * 64 + sm * 16, 16), 16)

    def rows64(yf):
        (fm, fd), (sm, sd) = axes(yf)
        return pl.ds(pl.multiple_of(fm * 64, 64), 64)

    def st4(ci, c):
        u0, n, yf = CHUNKS[ci]
        r16 = rows16(yf)
        @pl.when(jnp.logical_and(z >= u0, z < u0 + n))
        def _():
            zb[z] = h2[z]
            pltpu.make_async_copy(zb.at[pl.ds(0, 15)], zb.at[pl.ds(0, 15)], zr.at[ci // 2]).wait()
            tot = zb[0].astype(F32)
            for k in range(1, 16):
                tot = tot + zb[k].astype(F32)
            out[z, r16, mine] = tot.astype(BF16)
            for d in range(1, 16):
                to = lax.rem(z + d, 16)
                pltpu.make_async_remote_copy(src_ref=out.at[z, r16, mine], dst_ref=out.at[z, r16, mine], send_sem=gzs.at[ci // 2], recv_sem=gzr.at[z], device_id=dev(x, y, core, to), device_id_type=MESH).start()
        return None

    def st5(ci, c):
        u0, n, yf = CHUNKS[ci]
        us = pl.ds(u0, n)
        r16 = rows16(yf)
        for u in range(u0, u0 + n):
            @pl.when(z != u)
            def _():
                pltpu.make_async_copy(out.at[u, r16, mine], out.at[u, r16, mine], gzr.at[u]).wait()
        (fm, fd), (sm, sd) = axes(yf)
        return [push(out.at[us, r16, mine], out.at[us, r16, mine], g2s.at[ci, d - 1], g2r.at[ci, d - 1], sd(mod4(sm + d))) for d in range(1, 4)]

    def st6(ci, c):
        u0, n, yf = CHUNKS[ci]
        us = pl.ds(u0, n)
        for k in c:
            k.wait_recv()
        r64 = rows64(yf)
        (fm, fd), (sm, sd) = axes(yf)
        return [push(out.at[us, r64, mine], out.at[us, r64, mine], g1s.at[ci, d - 1], g1r.at[ci, d - 1], fd(mod4(fm + d))) for d in range(1, 4)]

    def st7(ci, c):
        u0, n, yf = CHUNKS[ci]
        us = pl.ds(u0, n)
        for k in c:
            k.wait_recv()
        return [push(out.at[us, :, mine], out.at[us, :, mine], g0s.at[ci], g0r.at[ci], sib)]


    state = [st0(0), st0(1), None, None]

    @pl.loop(0, 9)
    def _(t):
        rs = pl.ds(t * 2, 2)
        for b in range(3):
            s3[rs, :, b * 256 : b * 256 + 256] = sf[rs, 17 - b : 49 - b, :].astype(BF16)

    @pl.loop(0, 2)
    def _(t):
        acc = jnp.zeros((256, 256), F32)
        for a in range(3):
            for b in range(3):
                piece = s3[pl.ds(t * 8 + 2 - a, 8), :, b * 256 : b * 256 + 256].reshape(256, 256)
                acc += dot(piece, k2[a, b], ((1,), (1,)))
        ms[pl.ds(pl.multiple_of(t * 256, 256), 256)] = acc.astype(BF16)

    state[0] = st1(0, state[0])
    state[1] = st1(1, state[1])

    pack[11, 128:256, :] = dot(pool[2:18].reshape(512, 128), ms[...], ((0,), (0,))).astype(BF16)
    pack[11, 0:128, 128:256] = jnp.zeros((128, 128), BF16)

    @pl.loop(0, 4)
    def _(t):
        part = ms[pl.ds(pl.multiple_of(t * 128, 128), 128)]
        back = dot(part, proj[...], ((1,), (1,))).astype(BF16).astype(F32) * 0.25
        back = back.reshape(4, 32, 128)
        back = jnp.concatenate([back, back], axis=2)
        slope = d1[pl.ds(t * 8 + 4, 8)].reshape(4, 2, 32, 256)
        slope = jnp.stack([slope[:, 0] * back, slope[:, 1] * back], axis=1)
        s1[pl.ds(t * 8, 8)] = slope.reshape(8, 32, 256).astype(BF16)

    for a in range(3):
        grad = dot(xs[a + 4 : a + 36, 0:32].reshape(1024, 512), s1[...].reshape(1024, 256), ((0,), (0,)))
        for b in range(3):
            t = 3 * a + b
            tap = grad[b * 128 : b * 128 + 128, 0:128] + grad[b * 128 + 128 : b * 128 + 256, 128:256]
            pack[
                9 + t // 4, (t // 2) % 2 * 128 : (t // 2) % 2 * 128 + 128, t % 2 * 128 : t % 2 * 128 + 128
            ] = tap.astype(BF16)

    state[2], state[3] = st0(2), st0(3)
    state[0] = st2(0, state[0])
    state[1] = st2(1, state[1])
    state[2] = st1(2, state[2])
    state[3] = st1(3, state[3])
    for ci in range(4):
        state[ci] = (st3 if ci < 2 else st2)(ci, state[ci])
    for ci in range(4):
        state[ci] = (st4 if ci < 2 else st3)(ci, state[ci])
    for ci in range(4):
        state[ci] = (st5 if ci < 2 else st4)(ci, state[ci])
    for ci in range(4):
        state[ci] = (st6 if ci < 2 else st5)(ci, state[ci])
    for ci in range(4):
        state[ci] = (st7 if ci < 2 else st6)(ci, state[ci])
    for ci in (2, 3):
        state[ci] = st7(ci, state[ci])
    for c in state:
        for e in c:
            e.wait_recv()
    feat_copy.wait_recv()
    for c in sends:
        c.wait_send()
    for u in range(UNITS):
        @pl.when(z != u)
        def _():
            pltpu.make_async_copy(h2.at[u], h2.at[u], zs.at[u]).wait()
    for half, (lo, hi) in enumerate(((0, 9), (9, 12))):
        @pl.when(jnp.logical_and(z >= lo, z < hi))
        def _():
            pltpu.make_async_copy(zb.at[pl.ds(0, 15)], zb.at[pl.ds(0, 15)], gzs.at[half]).wait()


def network_call(img, k1, proj, k2, cot):
    V, D = pltpu.VMEM, pltpu.SemaphoreType.DMA
    n = len(CHUNKS)
    macs = 2 * 1000 * 1000 * 1000
    return pl.pallas_call(
        network,
        out_shape=(
            jax.ShapeDtypeStruct((UNITS, 256, 256), BF16),
            jax.ShapeDtypeStruct((16, 32, 256), BF16),
        ),
        in_specs=[pl.BlockSpec(memory_space=pltpu.VMEM)] * 5,
        out_specs=(pl.BlockSpec(memory_space=pltpu.VMEM),) * 2,
        scratch_shapes=[
            V((42, 112, 128), F32), V((42, 48, 512), BF16), V((3, 512, 256), BF16),
            V((40, 32, 256), F32), V((20, 32, 128), BF16), V((20, 64, 256), F32),
            V((20, 48, 768), BF16), V((18, 48, 256), F32), V((18, 64, 256), F32),
            V((18, 32, 256), BF16), V((18, 32, 768), BF16), V((512, 256), BF16),
            V((32, 32, 256), BF16), V((18, 32, 256), BF16), V((UNITS, 256, 256), BF16),
            V((2, 256, 128), BF16), V((2, 5, 64, 128), BF16), V((2, 256, 128), BF16),
            V((4, 48, 128), BF16), V((2, 16, 256), BF16), V((16, 32, 256), BF16),
            V((2, 32, 256), BF16), V((2, 3, 16, 256), BF16),
            V((UNITS, 256, 128), BF16), V((UNITS, 256, 128), BF16),
            V((3, UNITS, 64, 128), BF16), V((UNITS, 64, 128), BF16),
            V((3, UNITS, 16, 128), BF16), V((UNITS, 16, 128), BF16), V((16, 16, 128), BF16),
            D((8,)), D((8,)), D((9,)), D((9,)), D(()), D(()),
            D((n,)), D((n,)), D((n, 3)), D((n, 3)), D((n, 3)), D((n, 3)),
            D((UNITS,)), D((2,)), D((2,)), D((UNITS,)),
            D((n, 3)), D((n, 3)), D((n, 3)), D((n, 3)), D((n,)), D((n,)),
        ],
        compiler_params=pltpu.CompilerParams(
            collective_id=0, has_side_effects=True, vmem_limit_bytes=56 << 20
        ),
        cost_estimate=pl.CostEstimate(
            flops=2 * macs, bytes_accessed=8 << 20, transcendentals=1 << 20
        ),
    )(img, k1, proj, k2, cot)


def per_device(images, first_kernel, projection, second_kernel, cotangent):
    total, features = network_call(images[0], first_kernel, projection, second_kernel, cotangent[0])
    grad_second = total[:9].reshape(3, 3, 256, 256).astype(F32)
    blocks = total[9:].reshape(3, 2, 128, 2, 128).transpose(0, 1, 3, 2, 4).reshape(12, 128, 128)
    blocks = blocks.astype(F32)
    grad_first = blocks[:9].reshape(3, 3, 128, 128)
    grad_projection = jnp.concatenate([blocks[10], blocks[11]], axis=1)
    return (features[None], grad_first, grad_projection, grad_second)


def solution(mesh):
    placed = (P("section", "gy", "gx", None), P(), P(), P(), P("section", "gy", "gx", None))
    return jax.shard_map(
        per_device,
        mesh=mesh,
        in_specs=placed,
        out_specs=(P("section", "gy", "gx", None), P(), P(), P()),
        check_vma=False,
    )
```

time: 158 us -> 88.4 us (0.56)
  starting transfers between devices: 45.7 us -> 0 us
  waiting for transfers between devices: 24.1 us -> 0 us
  Pallas kernels: 58.4 us -> 80.8 us
  matrix products: 14.4 us -> 0 us
  other arithmetic: 7 us -> 3.35 us
  local copies, waits for them, and re-layouts: 6.48 us -> 3.39 us
    ppermute x14 -> x0, starting transfers between devices: 45.7 us -> none  [the longest x6 23.5 us: padded_2(): before = lax.ppermute(last, axis, up)]
    ppermute x14 -> x0, waiting for transfers between devices: 24.1 us -> none  [the longest x2 12.4 us: from_partner(): return lax.ppermute(block, axis, route)]
    pallas_call x1, Pallas kernels: 58.4 us -> 80.8 us  [network_call(): pl.pallas_call(network, out_shape=(jax.ShapeDtypeStruct((UNITS, 256, 256)...]
    dot_general x48 -> x0, matrix products: 14.4 us -> none  [the longest x18 5.76 us: conv_slopes(): jnp.einsum('pc,pd->cd', piece, slope, preferred_element_type=jnp.float32)]
    concatenate x6 -> x0, other arithmetic: 2.46 us -> none  [padded_2(): array = jnp.concatenate([before, array, after], axis=dim)]
  transfers between devices with their start and end apart: 14 -> 0, of which waited for: 8 -> 0; matrix products, arithmetic and copies ran while one was open for 3% -> 0% of each run, Pallas kernels for 0% -> 0%
where the time goes in v2:
time: 88.4 us; the launch traced here: 88.2 us
  Pallas kernels  80.8 us (91%)
  local copies, waits for them, and re-layouts  3.39 us (4%)
  other arithmetic  3.35 us (4%)
    pallas_call x1, Pallas kernels, network_call(): pl.pallas_call(network, out_shape=(jax.ShapeDtypeStruct((UNITS, 256, 256)...  80.8 us

profile of v2, /device:TPU:1, one launch (start us, length us, event | category | flops | bytes accessed | tf_op | source)
XLA Modules:
  0.0 88.2 jit_solution(1506013518558907358)
XLA Ops:
  0.6 80.8 %shard_map.84 = (bf16[12,256,256]{2,1,0:T(8,128)(2,1)}, bf16[16,32,256]{2,1,0:T(8,128)(2,1)}) custom-call(bf16[32,64,128]{2,1,0:T(8,128)(2,1)} %bitcast.18, bf16[3,3,128,128]{3,2,1,0:T(8,128)(2,1)} %k1.1, bf16[128,256]{1,0:T(8,128)(2,1)} %proj.1, bf16[3,3,256,256]{3,2,1,0:T(8,128)(2,1)} %k2.1, bf16[16,32,256]{2,1,0:T(8,128)(2,1)} %bitcast.19), custom_call_target="tpu_custom_call" | custom-call | flops 4000000000 | bytes 8388608 | tf_op jit(solution)/shard_map/pallas_call | solution.py:420
  81.4 1.1 %slice_convert_fusion = f32[3,256,256]{2,1,0:T(8,128)S(1)} fusion(bf16[12,256,256]{2,1,0:T(8,128)(2,1)} %get-tuple-element.7), kind=kLoop, calls=%fused_computation | loop fusion | flops 196608 | bytes 1179648 | tf_op jit(solution)/shard_map/convert_element_type | solution.py:458
  82.5 1.3 %slice.19 = bf16[9,256,256]{2,1,0:T(8,128)(2,1)S(1)} slice(bf16[12,256,256]{2,1,0:T(8,128)(2,1)} %get-tuple-element.7), slice={[0:9], [0:256], [0:256]} | slice | bytes 2359296 | tf_op jit(solution)/shard_map/slice | solution.py:456
  83.9 0.4 reshape.23
  84.3 0.1 copy.9
  84.4 0.9 slice.20
  85.2 0.7 pad_maximum_fusion
  85.9 0.0 copy-start
  85.9 1.6 %convert.4 = f32[3,3,256,256]{3,2,1,0:T(8,128)} convert(bf16[3,3,256,256]{3,2,1,0:T(8,128)(2,1)S(1)} %bitcast.12) | non-fusion elementwise | flops 589824 | bytes 3538944 | tf_op jit(solution)/shard_map/convert_element_type | solution.py:456
  87.5 0.0 copy-done
  87.5 0.7 copy.11
  (1 shorter events, 0.0 us)
Async XLA Ops:
  85.9 1.6 %copy-start = (bf16[16,32,256]{2,1,0:T(8,128)(2,1)S(1)}, bf16[16,32,256]{2,1,0:T(8,128)(2,1)}, u32[]{:S(2)}) copy-start(bf16[16,32,256]{2,1,0:T(8,128)(2,1)} %get-tuple-element.6) | copy-start | bytes 786436

commit v3 on v2

--- a/solution.py
+++ b/solution.py
@@ -10,7 +10,7 @@
 MESH = pl.DeviceIdType.MESH
 F32, BF16 = jnp.float32, jnp.bfloat16
 UNITS = 12
-CHUNKS = ((0, 5, True), (5, 4, False), (9, 1, True), (10, 2, False))
+CHUNKS = ((0, 4, True), (4, 4, False), (8, 2, True), (10, 2, False))
 AROUND = ((-1, 0), (1, 0), (0, -1), (0, 1), (-1, -1), (-1, 1), (1, -1), (1, 1))
 
 
@@ -38,12 +38,13 @@
 
 
 def network(
-    img, k1, proj, k2, cot, out, feat,
+    img_in, k1_in, proj_in, k2_in, cot_h, out, feat,
+    img, k1, proj, k2, cot, fetch,
     xf, xs, w1, d1, pool, mf, m3, cotf, sf, si, s3, ms, s1, fb, pack,
     colpack, rows_in, cols_in, corners_in, cotpack, cot_in, cot_rows, cot_cols,
-    r0, h0, r1, h1, r2, h2, zb,
+    r0, h0, r1, h1, r2, h2, ra, hz, rb0, rl, rb1,
     hs, hr, cs, cr, fs, fr,
-    s0s, s0r, s1s, s1r, s2s, s2r, zs, zr, gzs, gzr, g2s, g2r, g1s, g1r, g0s, g0r,
+    s0s, s0r, s1s, s1r, s2s, s2r, zas, zar, zbs, zbr, zcs, zcr, g2s, g2r, g1s, g1r, g0s, g0r, ready,
 ):
     x, y, core, z = coords()
     sec, gy = lax.axis_index("section"), lax.axis_index("gy")
@@ -66,17 +67,33 @@
     for d in range(1, 4):
         greet(dev(mod4(x + d), y, core, z))
         greet(dev(x, mod4(y + d), core, z))
-    for d in range(1, 16):
-        greet(dev(x, y, core, lax.rem(z + d, 16)))
-
+    zl, zh = mod4(z), lax.div(z, 4)
+    for d in range(1, 4):
+        greet(dev(x, y, core, zh * 4 + mod4(zl + d)))
+    greet(dev(x, y, core, lax.rem(z + 4, 16)))
+    greet(dev(x, y, core, lax.rem(z + 12, 16)))
+
+    fetches = [
+        pltpu.make_async_copy(src, dst, fetch.at[i])
+        for i, (src, dst) in enumerate(
+            ((img_in, img), (cot_h, cot), (k1_in, k1), (proj_in, proj), (k2_in, k2))
+        )
+    ]
+    for c in fetches:
+        c.start()
+    fetches[0].wait()
     xf[5:37, 24:88] = img[...].astype(F32)
     colpack[0] = xf[5:37, 24:32].reshape(256, 128).astype(BF16)
     colpack[1] = xf[5:37, 80:88].reshape(256, 128).astype(BF16)
+    fetches[1].wait()
     cotf[0:16, 0:32] = cot[...].astype(F32)
     cotpack[0] = cotf[0:16, 0, :].astype(BF16)
     cotpack[1] = cotf[0:16, 31, :].astype(BF16)
 
-    pl.semaphore_wait(barrier, 39)
+    pl.semaphore_wait(barrier, 29)
+    pl.semaphore_signal(
+        ready, inc=1, device_id=dev(x, y, core, lax.rem(z + 12, 16)), device_id_type=MESH
+    )
     sends = []
 
     def push(src, dst, ss, rs, to):
@@ -109,6 +126,7 @@
         push(cotpack.at[1], cot_cols.at[0, 0], cs.at[8], cr.at[8], near(other_sec, 1, 1)),
     ]
 
+    fetches[2].wait()
     zero = jnp.zeros((128, 128), BF16)
     for a in range(3):
         w1[a, 384:512, 0:128] = zero
@@ -122,6 +140,8 @@
     mf[:, 56:64] = jnp.zeros((20, 8, 256), F32)
     cotf[...] = jnp.zeros((18, 48, 256), F32)
 
+    fetches[3].wait()
+    fetches[4].wait()
     for c in halo:
         c.wait_recv()
     xf[0:5, 24:88] = rows_in[0].astype(F32)
@@ -280,11 +300,6 @@
             k.wait_recv()
         (fm, fd), (sm, sd) = axes(yf)
         h2[us] = (h1[us, pl.ds(pl.multiple_of(sm * 16, 16), 16)].astype(F32) + r2[0, us].astype(F32) + r2[1, us].astype(F32) + r2[2, us].astype(F32)).astype(BF16)
-        for u in range(u0, u0 + n):
-            @pl.when(z != u)
-            def _():
-                pltpu.make_async_remote_copy(src_ref=h2.at[u], dst_ref=zb.at[z], send_sem=zs.at[u], recv_sem=zr.at[ci // 2], device_id=dev(x, y, core, u), device_id_type=MESH).start()
-        return None
 
     def rows16(yf):
         (fm, fd), (sm, sd) = axes(yf)
@@ -294,30 +309,61 @@
         (fm, fd), (sm, sd) = axes(yf)
         return pl.ds(pl.multiple_of(fm * 64, 64), 64)
 
-    def st4(ci, c):
-        u0, n, yf = CHUNKS[ci]
+    def run(d):
+        return dev(x, y, core, zh * 4 + mod4(zl + d))
+
+    def za0():
+        out_c = []
+        for d in range(1, 4):
+            p = mod4(zl + d)
+            out_c.append(push(h2.at[pl.ds(p * 2, 2)], ra.at[d - 1], zas.at[0, d - 1], zar.at[0, d - 1], run(d)))
+        return out_c
+
+    def za1():
+        rl[zl] = h2[8:12]
+        return [push(h2.at[8:12], rl.at[zl], zas.at[1, d - 1], zar.at[1, d - 1], run(d)) for d in range(1, 4)]
+
+    def far(src, dst, zi):
+        return [push(src, dst, zbs.at[zi, d - 1], zbr.at[zi, d - 1], dev(x, y, core, lax.rem(z + 4 * d, 16))) for d in (2, 1, 3)]
+
+    def sum4(ref):
+        return ref[0].astype(F32) + ref[1].astype(F32) + ref[2].astype(F32) + ref[3].astype(F32)
+
+    def zb0(c):
+        for k in c:
+            k.wait_recv()
+        hz[0:2] = (h2[pl.ds(zl * 2, 2)].astype(F32) + ra[0].astype(F32) + ra[1].astype(F32) + ra[2].astype(F32)).astype(BF16)
+        rb0[zh] = hz[0:2]
+        pl.semaphore_wait(ready, 1)
+        return far(hz.at[0:2], rb0.at[zh], 0)
+
+    def zb1(c):
+        for k in c:
+            k.wait_recv()
+        hz[2:6] = sum4(rl).astype(BF16)
+        rb1[zh] = hz[2:6]
+        return far(hz.at[2:6], rb1.at[zh], 1)
+
+    def zc0(c):
+        for k in c:
+            k.wait_recv()
+        flag = lax.div(zl, 2)
+        r16 = pl.ds(pl.multiple_of((1 - flag) * (y * 64 + x * 16) + flag * (x * 64 + y * 16), 16), 16)
+        us = pl.ds(zl * 2, 2)
+        out[us, r16, mine] = sum4(rb0).astype(BF16)
+        return [push(out.at[us, r16, mine], out.at[us, r16, mine], zcs.at[d - 1], zcr.at[d - 1], run(d)) for d in range(1, 4)]
+
+    def zc1(c):
+        for k in c:
+            k.wait_recv()
+        total = sum4(rb1).astype(BF16)
+        out[8:10, rows16(True), mine] = total[0:2]
+        out[10:12, rows16(False), mine] = total[2:4]
+
+    def st5(ci):
+        u0, n, yf = CHUNKS[ci]
+        us = pl.ds(u0, n)
         r16 = rows16(yf)
-        @pl.when(jnp.logical_and(z >= u0, z < u0 + n))
-        def _():
-            zb[z] = h2[z]
-            pltpu.make_async_copy(zb.at[pl.ds(0, 15)], zb.at[pl.ds(0, 15)], zr.at[ci // 2]).wait()
-            tot = zb[0].astype(F32)
-            for k in range(1, 16):
-                tot = tot + zb[k].astype(F32)
-            out[z, r16, mine] = tot.astype(BF16)
-            for d in range(1, 16):
-                to = lax.rem(z + d, 16)
-                pltpu.make_async_remote_copy(src_ref=out.at[z, r16, mine], dst_ref=out.at[z, r16, mine], send_sem=gzs.at[ci // 2], recv_sem=gzr.at[z], device_id=dev(x, y, core, to), device_id_type=MESH).start()
-        return None
-
-    def st5(ci, c):
-        u0, n, yf = CHUNKS[ci]
-        us = pl.ds(u0, n)
-        r16 = rows16(yf)
-        for u in range(u0, u0 + n):
-            @pl.when(z != u)
-            def _():
-                pltpu.make_async_copy(out.at[u, r16, mine], out.at[u, r16, mine], gzr.at[u]).wait()
         (fm, fd), (sm, sd) = axes(yf)
         return [push(out.at[us, r16, mine], out.at[us, r16, mine], g2s.at[ci, d - 1], g2r.at[ci, d - 1], sd(mod4(sm + d))) for d in range(1, 4)]
 
@@ -385,32 +431,32 @@
     state[1] = st2(1, state[1])
     state[2] = st1(2, state[2])
     state[3] = st1(3, state[3])
-    for ci in range(4):
-        state[ci] = (st3 if ci < 2 else st2)(ci, state[ci])
-    for ci in range(4):
-        state[ci] = (st4 if ci < 2 else st3)(ci, state[ci])
-    for ci in range(4):
-        state[ci] = (st5 if ci < 2 else st4)(ci, state[ci])
-    for ci in range(4):
-        state[ci] = (st6 if ci < 2 else st5)(ci, state[ci])
-    for ci in range(4):
-        state[ci] = (st7 if ci < 2 else st6)(ci, state[ci])
-    for ci in (2, 3):
-        state[ci] = st7(ci, state[ci])
+    st3(0, state[0])
+    st3(1, state[1])
+    first = za0()
+    state[2] = st2(2, state[2])
+    state[3] = st2(3, state[3])
+    first = zb0(first)
+    st3(2, state[2])
+    st3(3, state[3])
+    second = za1()
+    second = zb1(second)
+    first = zc0(first)
+    for c in first:
+        c.wait_recv()
+    state[0], state[1] = st5(0), st5(1)
+    zc1(second)
+    state[2], state[3] = st5(2), st5(3)
+    state[0], state[1] = st6(0, state[0]), st6(1, state[1])
+    state[2], state[3] = st6(2, state[2]), st6(3, state[3])
+    state[0], state[1] = st7(0, state[0]), st7(1, state[1])
+    state[2], state[3] = st7(2, state[2]), st7(3, state[3])
     for c in state:
         for e in c:
             e.wait_recv()
     feat_copy.wait_recv()
     for c in sends:
         c.wait_send()
-    for u in range(UNITS):
-        @pl.when(z != u)
-        def _():
-            pltpu.make_async_copy(h2.at[u], h2.at[u], zs.at[u]).wait()
-    for half, (lo, hi) in enumerate(((0, 9), (9, 12))):
-        @pl.when(jnp.logical_and(z >= lo, z < hi))
-        def _():
-            pltpu.make_async_copy(zb.at[pl.ds(0, 15)], zb.at[pl.ds(0, 15)], gzs.at[half]).wait()
 
 
 def network_call(img, k1, proj, k2, cot):
@@ -423,9 +469,11 @@
             jax.ShapeDtypeStruct((UNITS, 256, 256), BF16),
             jax.ShapeDtypeStruct((16, 32, 256), BF16),
         ),
-        in_specs=[pl.BlockSpec(memory_space=pltpu.VMEM)] * 5,
+        in_specs=[pl.BlockSpec(memory_space=pltpu.HBM)] * 5,
         out_specs=(pl.BlockSpec(memory_space=pltpu.VMEM),) * 2,
         scratch_shapes=[
+            V((32, 64, 128), BF16), V((3, 3, 128, 128), BF16), V((128, 256), BF16),
+            V((3, 3, 256, 256), BF16), V((16, 32, 256), BF16), D((5,)),
             V((42, 112, 128), F32), V((42, 48, 512), BF16), V((3, 512, 256), BF16),
             V((40, 32, 256), F32), V((20, 32, 128), BF16), V((20, 64, 256), F32),
             V((20, 48, 768), BF16), V((18, 48, 256), F32), V((18, 64, 256), F32),
@@ -436,11 +484,14 @@
             V((2, 32, 256), BF16), V((2, 3, 16, 256), BF16),
             V((UNITS, 256, 128), BF16), V((UNITS, 256, 128), BF16),
             V((3, UNITS, 64, 128), BF16), V((UNITS, 64, 128), BF16),
-            V((3, UNITS, 16, 128), BF16), V((UNITS, 16, 128), BF16), V((16, 16, 128), BF16),
+            V((3, UNITS, 16, 128), BF16), V((UNITS, 16, 128), BF16),
+            V((3, 2, 16, 128), BF16), V((6, 16, 128), BF16), V((4, 2, 16, 128), BF16),
+            V((4, 4, 16, 128), BF16), V((4, 4, 16, 128), BF16),
             D((8,)), D((8,)), D((9,)), D((9,)), D(()), D(()),
             D((n,)), D((n,)), D((n, 3)), D((n, 3)), D((n, 3)), D((n, 3)),
-            D((UNITS,)), D((2,)), D((2,)), D((UNITS,)),
+            D((2, 3)), D((2, 3)), D((2, 3)), D((2, 3)), D((3,)), D((3,)),
             D((n, 3)), D((n, 3)), D((n, 3)), D((n, 3)), D((n,)), D((n,)),
+            pltpu.SemaphoreType.REGULAR,
         ],
         compiler_params=pltpu.CompilerParams(
             collective_id=0, has_side_effects=True, vmem_limit_bytes=56 << 20
@@ -451,14 +502,31 @@
     )(img, k1, proj, k2, cot)
 
 
+def widen(total, near, features, grad_first, grad_projection, grad_second):
+    features[0] = near[...]
+    for t in range(9):
+        a, b = t // 3, t % 3
+        row, lane = (t // 2) % 2 * 128, t % 2 * 128
+        grad_second[a, b] = total[t].astype(F32)
+        grad_first[a, b] = total[9 + t // 4, row : row + 128, lane : lane + 128].astype(F32)
+    grad_projection[...] = total[11, 128:256, :].astype(F32)
+
+
 def per_device(images, first_kernel, projection, second_kernel, cotangent):
     total, features = network_call(images[0], first_kernel, projection, second_kernel, cotangent[0])
-    grad_second = total[:9].reshape(3, 3, 256, 256).astype(F32)
-    blocks = total[9:].reshape(3, 2, 128, 2, 128).transpose(0, 1, 3, 2, 4).reshape(12, 128, 128)
-    blocks = blocks.astype(F32)
-    grad_first = blocks[:9].reshape(3, 3, 128, 128)
-    grad_projection = jnp.concatenate([blocks[10], blocks[11]], axis=1)
-    return (features[None], grad_first, grad_projection, grad_second)
+    features, grad_first, grad_projection, grad_second = pl.pallas_call(
+        widen,
+        out_shape=(
+            jax.ShapeDtypeStruct((1, 16, 32, 256), BF16),
+            jax.ShapeDtypeStruct((3, 3, 128, 128), F32),
+            jax.ShapeDtypeStruct((128, 256), F32),
+            jax.ShapeDtypeStruct((3, 3, 256, 256), F32),
+        ),
+        in_specs=[pl.BlockSpec(memory_space=pltpu.VMEM)] * 2,
+        out_specs=(pl.BlockSpec(memory_space=pltpu.VMEM),) * 4,
+        compiler_params=pltpu.CompilerParams(vmem_limit_bytes=24 << 20),
+    )(total, features)
+    return (features, grad_first, grad_projection, grad_second)
 
 
 def solution(mesh):

time: 88.4 us -> 77.2 us (0.87)
  Pallas kernels: 80.8 us -> 74 us
  other arithmetic: 3.35 us -> 0 us
  local copies, waits for them, and re-layouts: 3.39 us -> 2.35 us
    pallas_call x1, Pallas kernels: 80.8 us -> 72.1 us  [network_call(): pl.pallas_call(network, out_shape=(jax.ShapeDtypeStruct((UNITS, 256, 256)...]
    convert_element_type x2 -> x0, other arithmetic: 2.69 us -> none  [the longest x1 1.63 us: per_device(): grad_second = total[:9].reshape(3, 3, 256, 256).astype(F32)]
    slice x2 -> x0, local copies, waits for them, and re-layouts: 2.21 us -> none  [the longest x1 1.35 us: per_device(): grad_second = total[:9].reshape(3, 3, 256, 256).astype(F32)]
    pallas_call x0 -> x1, Pallas kernels: none -> 1.87 us  [per_device(): pl.pallas_call(widen, out_shape=(jax.ShapeDtypeStruct((1, 16, 32, 256), B...]
    unnamed x3 -> x4, local copies, waits for them, and re-layouts: 0.71 us -> 2.35 us
where the time goes in v3:
time: 77.2 us; the launch traced here: 77 us
  Pallas kernels  74 us (96%)
  local copies, waits for them, and re-layouts  2.35 us (3%)
    pallas_call x1, Pallas kernels, network_call(): pl.pallas_call(network, out_shape=(jax.ShapeDtypeStruct((UNITS, 256, 256)...  72.1 us
    unnamed x4, local copies, waits for them, and re-layouts  2.35 us
    pallas_call x1, Pallas kernels, per_device(): pl.pallas_call(widen, out_shape=(jax.ShapeDtypeStruct((1, 16, 32, 256), B...  1.87 us

profile of v3, /device:TPU:1, one launch (start us, length us, event | category | flops | bytes accessed | tf_op | source)
XLA Modules:
  0.0 77.0 jit_solution(14123038562677798572)
XLA Ops:
  0.6 72.1 %shard_map.84 = (bf16[12,256,256]{2,1,0:T(8,128)(2,1)}, bf16[16,32,256]{2,1,0:T(8,128)(2,1)}) custom-call(bf16[32,64,128]{2,1,0:T(8,128)(2,1)} %bitcast.2, bf16[3,3,128,128]{3,2,1,0:T(8,128)(2,1)} %k1_in.1, bf16[128,256]{1,0:T(8,128)(2,1)} %proj_in.1, bf16[3,3,256,256]{3,2,1,0:T(8,128)(2,1)} %k2_in.1, bf16[16,32,256]{2,1,0:T(8,128)(2,1)} %bitcast.3), custom_call_target="tpu_custom_call" | custom-call | flops 4000000000 | bytes 8388608 | tf_op jit(solution)/shard_map/pallas_call | solution.py:466
  72.8 0.0 copy-start
  72.8 1.4 %copy-done = bf16[12,256,256]{2,1,0:T(8,128)(2,1)S(1)} copy-done((bf16[12,256,256]{2,1,0:T(8,128)(2,1)S(1)}, bf16[12,256,256]{2,1,0:T(8,128)(2,1)}, u32[]{:S(2)}) %copy-start) | copy-done | bytes 1572888
  74.2 0.0 copy-start.1
  74.2 0.9 %copy-done.1 = bf16[16,32,256]{2,1,0:T(8,128)(2,1)S(1)} copy-done((bf16[16,32,256]{2,1,0:T(8,128)(2,1)S(1)}, bf16[16,32,256]{2,1,0:T(8,128)(2,1)}, u32[]{:S(2)}) %copy-start.1) | copy-done | bytes 262168
  75.1 1.9 %shard_map.85 = (bf16[1,16,32,256]{3,2,1,0:T(8,128)(2,1)}, f32[3,3,128,128]{3,2,1,0:T(8,128)}, f32[128,256]{1,0:T(8,128)}, f32[3,3,256,256]{3,2,1,0:T(8,128)}) custom-call(bf16[12,256,256]{2,1,0:T(8,128)(2,1)S(1)} %copy-done, bf16[16,32,256]{2,1,0:T(8,128)(2,1)S(1)} %copy-done.1), custom_call_target="tpu_custom_call" | custom-call | tf_op jit(solution)/shard_map/pallas_call | solution.py:517
Async XLA Ops:
  72.8 1.4 %copy-start = (bf16[12,256,256]{2,1,0:T(8,128)(2,1)S(1)}, bf16[12,256,256]{2,1,0:T(8,128)(2,1)}, u32[]{:S(2)}) copy-start(bf16[12,256,256]{2,1,0:T(8,128)(2,1)} %get-tuple-element.6.total) | copy-start | bytes 4718596
  74.2 0.9 %copy-start.1 = (bf16[16,32,256]{2,1,0:T(8,128)(2,1)S(1)}, bf16[16,32,256]{2,1,0:T(8,128)(2,1)}, u32[]{:S(2)}) copy-start(bf16[16,32,256]{2,1,0:T(8,128)(2,1)} %get-tuple-element.7.near) | copy-start | bytes 786436

commit v4 on v3

--- a/solution.py
+++ b/solution.py
@@ -38,9 +38,10 @@
 
 
 def network(
-    img_in, k1_in, proj_in, k2_in, cot_h, out, feat,
+    img_in, k1_in, proj_in, k2_in, cot_h, out_h, feat,
+    out, leave,
     img, k1, proj, k2, cot, fetch,
-    xf, xs, w1, d1, pool, mf, m3, cotf, sf, si, s3, ms, s1, fb, pack,
+    xf, xs, w1, d1, pool, mf, m3, cotf, slopes, sf, si, s3, ms, s1, fb, pack,
     colpack, rows_in, cols_in, corners_in, cotpack, cot_in, cot_rows, cot_cols,
     r0, h0, r1, h1, r2, h2, ra, hz, rb0, rl, rb1,
     hs, hr, cs, cr, fs, fr,
@@ -207,6 +208,17 @@
             sides = [mf[rs, 47 + b : 55 + b, :], mf[rs, 7 + b : 15 + b, :]]
             m3[rs, 32:48, lanes] = jnp.concatenate(sides, axis=1).astype(BF16)
 
+    @pl.loop(0, 3)
+    def _(t):
+        acc = dot(m3[pl.ds(t * 6, 6)].reshape(288, 768), k2[0].reshape(768, 256))
+        acc += dot(m3[pl.ds(t * 6 + 1, 6)].reshape(288, 768), k2[1].reshape(768, 256))
+        acc += dot(m3[pl.ds(t * 6 + 2, 6)].reshape(288, 768), k2[2].reshape(768, 256))
+        sig = sigmoid(acc)
+        fb[pl.ds(t * 6, 6)] = (acc * sig).astype(BF16).reshape(6, 48, 256)[:, 0:32]
+        slopes[pl.ds(t * 6, 6)] = (sig * (1.0 + acc * (1.0 - sig))).reshape(6, 48, 256)
+
+    feat_copy = push(fb.at[1:17], feat, fs, fr, near(other_sec, 0, 0))
+
     for c in cots:
         c.wait_recv()
     cotf[1:17, 0:32] = cot_in[...].astype(F32)
@@ -237,19 +249,12 @@
 
     @pl.loop(0, 3)
     def _(t):
-        acc = dot(m3[pl.ds(t * 6, 6)].reshape(288, 768), k2[0].reshape(768, 256))
-        acc += dot(m3[pl.ds(t * 6 + 1, 6)].reshape(288, 768), k2[1].reshape(768, 256))
-        acc += dot(m3[pl.ds(t * 6 + 2, 6)].reshape(288, 768), k2[2].reshape(768, 256))
-        sig = sigmoid(acc)
-        fb[pl.ds(t * 6, 6)] = (acc * sig).astype(BF16).reshape(6, 48, 256)[:, 0:32]
-        slope = (sig * (1.0 + acc * (1.0 - sig))).reshape(6, 48, 256) * cotf[pl.ds(t * 6, 6)]
-        slope = slope.astype(BF16)
+        slope = (slopes[pl.ds(t * 6, 6)] * cotf[pl.ds(t * 6, 6)]).astype(BF16)
         si[pl.ds(t * 6, 6)] = slope[:, 0:32]
         slope = slope.astype(F32)
         sf[pl.ds(t * 6, 6), 16:56] = slope[:, 0:40]
         sf[pl.ds(t * 6, 6), 8:16] = slope[:, 40:48]
 
-    feat_copy = push(fb.at[1:17], feat, fs, fr, near(other_sec, 0, 0))
 
     for a in range(3):
         grad = dot(m3[a + 1 : a + 17, 0:32].reshape(512, 768), si[1:17].reshape(512, 256), ((0,), (0,)))
@@ -451,9 +456,16 @@
     state[2], state[3] = st6(2, state[2]), st6(3, state[3])
     state[0], state[1] = st7(0, state[0]), st7(1, state[1])
     state[2], state[3] = st7(2, state[2]), st7(3, state[3])
-    for c in state:
-        for e in c:
-            e.wait_recv()
+    leaves = []
+    for half, (u, n) in enumerate(((0, 8), (8, 4))):
+        for c in state[2 * half : 2 * half + 2]:
+            for e in c:
+                e.wait_recv()
+        c = pltpu.make_async_copy(out.at[u : u + n], out_h.at[u : u + n], leave.at[half])
+        c.start()
+        leaves.append(c)
+    for c in leaves:
+        c.wait()
     feat_copy.wait_recv()
     for c in sends:
         c.wait_send()
@@ -470,13 +482,14 @@
             jax.ShapeDtypeStruct((16, 32, 256), BF16),
         ),
         in_specs=[pl.BlockSpec(memory_space=pltpu.HBM)] * 5,
-        out_specs=(pl.BlockSpec(memory_space=pltpu.VMEM),) * 2,
+        out_specs=(pl.BlockSpec(memory_space=pltpu.HBM),) * 2,
         scratch_shapes=[
+            V((UNITS, 256, 256), BF16), D((2,)),
             V((32, 64, 128), BF16), V((3, 3, 128, 128), BF16), V((128, 256), BF16),
             V((3, 3, 256, 256), BF16), V((16, 32, 256), BF16), D((5,)),
             V((42, 112, 128), F32), V((42, 48, 512), BF16), V((3, 512, 256), BF16),
             V((40, 32, 256), F32), V((20, 32, 128), BF16), V((20, 64, 256), F32),
-            V((20, 48, 768), BF16), V((18, 48, 256), F32), V((18, 64, 256), F32),
+            V((20, 48, 768), BF16), V((18, 48, 256), F32), V((18, 48, 256), F32), V((18, 64, 256), F32),
             V((18, 32, 256), BF16), V((18, 32, 768), BF16), V((512, 256), BF16),
             V((32, 32, 256), BF16), V((18, 32, 256), BF16), V((UNITS, 256, 256), BF16),
             V((2, 256, 128), BF16), V((2, 5, 64, 128), BF16), V((2, 256, 128), BF16),
@@ -502,14 +515,40 @@
     )(img, k1, proj, k2, cot)
 
 
-def widen(total, near, features, grad_first, grad_projection, grad_second):
-    features[0] = near[...]
+def widen(
+    total, near, features, grad_first, grad_projection, grad_second,
+    narrow, first, projection, second, feat, in_sems, out_sems,
+):
+    cuts = ((9, 3), (0, 3), (3, 3), (6, 3))
+    loads = [
+        pltpu.make_async_copy(total.at[u : u + n], narrow.at[u : u + n], in_sems.at[i])
+        for i, (u, n) in enumerate(cuts)
+    ] + [pltpu.make_async_copy(near, feat, in_sems.at[4])]
+    for c in loads:
+        c.start()
+    stores = []
+
+    def store(src, dst):
+        c = pltpu.make_async_copy(src, dst, out_sems.at[len(stores)])
+        c.start()
+        stores.append(c)
+
+    loads[0].wait()
     for t in range(9):
-        a, b = t // 3, t % 3
         row, lane = (t // 2) % 2 * 128, t % 2 * 128
-        grad_second[a, b] = total[t].astype(F32)
-        grad_first[a, b] = total[9 + t // 4, row : row + 128, lane : lane + 128].astype(F32)
-    grad_projection[...] = total[11, 128:256, :].astype(F32)
+        first[t // 3, t % 3] = narrow[9 + t // 4, row : row + 128, lane : lane + 128].astype(F32)
+    projection[...] = narrow[11, 128:256, :].astype(F32)
+    store(first, grad_first)
+    store(projection, grad_projection)
+    for a in range(3):
+        loads[1 + a].wait()
+        for b in range(3):
+            second[a, b] = narrow[3 * a + b].astype(F32)
+        store(second.at[a], grad_second.at[a])
+    loads[4].wait()
+    store(feat, features.at[0])
+    for c in stores:
+        c.wait()
 
 
 def per_device(images, first_kernel, projection, second_kernel, cotangent):
@@ -522,9 +561,15 @@
             jax.ShapeDtypeStruct((128, 256), F32),
             jax.ShapeDtypeStruct((3, 3, 256, 256), F32),
         ),
-        in_specs=[pl.BlockSpec(memory_space=pltpu.VMEM)] * 2,
-        out_specs=(pl.BlockSpec(memory_space=pltpu.VMEM),) * 4,
-        compiler_params=pltpu.CompilerParams(vmem_limit_bytes=24 << 20),
+        in_specs=[pl.BlockSpec(memory_space=pltpu.HBM)] * 2,
+        out_specs=(pl.BlockSpec(memory_space=pltpu.HBM),) * 4,
+        scratch_shapes=[
+            pltpu.VMEM((UNITS, 256, 256), BF16), pltpu.VMEM((3, 3, 128, 128), F32),
+            pltpu.VMEM((128, 256), F32), pltpu.VMEM((3, 3, 256, 256), F32),
+            pltpu.VMEM((16, 32, 256), BF16),
+            pltpu.SemaphoreType.DMA((5,)), pltpu.SemaphoreType.DMA((6,)),
+        ],
+        compiler_params=pltpu.CompilerParams(vmem_limit_bytes=60 << 20),
     )(total, features)
     return (features, grad_first, grad_projection, grad_second)
 

time: 77.2 us -> 73.8 us (0.956)
  local copies, waits for them, and re-layouts: 2.35 us -> 0 us
  Pallas kernels: 74 us -> 73 us
    unnamed x4 -> x0, local copies, waits for them, and re-layouts: 2.35 us -> none
    pallas_call x1, Pallas kernels: 72.1 us -> 70.2 us  [network_call(): pl.pallas_call(network, out_shape=(jax.ShapeDtypeStruct((UNITS, 256, 256)...]
    pallas_call x1, Pallas kernels: 1.87 us -> 2.85 us  [per_device(): pl.pallas_call(widen, out_shape=(jax.ShapeDtypeStruct((1, 16, 32, 256), B...]
where the time goes in v4:
time: 73.8 us; the launch traced here: 73.7 us
  Pallas kernels  73 us (99%)
    pallas_call x1, Pallas kernels, network_call(): pl.pallas_call(network, out_shape=(jax.ShapeDtypeStruct((UNITS, 256, 256)...  70.2 us
    pallas_call x1, Pallas kernels, per_device(): pl.pallas_call(widen, out_shape=(jax.ShapeDtypeStruct((1, 16, 32, 256), B...  2.85 us

profile of v4, /device:TPU:1, one launch (start us, length us, event | category | flops | bytes accessed | tf_op | source)
XLA Modules:
  0.0 73.7 jit_solution(659091289336310129)
XLA Ops:
  0.6 70.2 %shard_map.84 = (bf16[12,256,256]{2,1,0:T(8,128)(2,1)}, bf16[16,32,256]{2,1,0:T(8,128)(2,1)}) custom-call(bf16[32,64,128]{2,1,0:T(8,128)(2,1)} %bitcast.2, bf16[3,3,128,128]{3,2,1,0:T(8,128)(2,1)} %k1_in.1, bf16[128,256]{1,0:T(8,128)(2,1)} %proj_in.1, bf16[3,3,256,256]{3,2,1,0:T(8,128)(2,1)} %k2_in.1, bf16[16,32,256]{2,1,0:T(8,128)(2,1)} %bitcast.3), custom_call_target="tpu_custom_call" | custom-call | flops 4000000000 | bytes 8388608 | tf_op jit(solution)/shard_map/pallas_call | solution.py:478
  70.8 2.8 %shard_map.85 = (bf16[1,16,32,256]{3,2,1,0:T(8,128)(2,1)}, f32[3,3,128,128]{3,2,1,0:T(8,128)}, f32[128,256]{1,0:T(8,128)}, f32[3,3,256,256]{3,2,1,0:T(8,128)}) custom-call(bf16[12,256,256]{2,1,0:T(8,128)(2,1)} %get-tuple-element.6.total, bf16[16,32,256]{2,1,0:T(8,128)(2,1)} %get-tuple-element.7.near), custom_call_target="tpu_custom_call" | custom-call | tf_op jit(solution)/shard_map/pallas_call | solution.py:556

commit v5 on v4

--- a/solution.py
+++ b/solution.py
@@ -217,7 +217,6 @@
         fb[pl.ds(t * 6, 6)] = (acc * sig).astype(BF16).reshape(6, 48, 256)[:, 0:32]
         slopes[pl.ds(t * 6, 6)] = (sig * (1.0 + acc * (1.0 - sig))).reshape(6, 48, 256)
 
-    feat_copy = push(fb.at[1:17], feat, fs, fr, near(other_sec, 0, 0))
 
     for c in cots:
         c.wait_recv()
@@ -445,6 +444,7 @@
     st3(2, state[2])
     st3(3, state[3])
     second = za1()
+    feat_copy = push(fb.at[1:17], feat, fs, fr, near(other_sec, 0, 0))
     second = zb1(second)
     first = zc0(first)
     for c in first:

time: 73.8 us -> 71 us (0.962)
  Pallas kernels: 73 us -> 70.1 us
    pallas_call x1, Pallas kernels: 70.2 us -> 67.3 us  [network_call(): pl.pallas_call(network, out_shape=(jax.ShapeDtypeStruct((UNITS, 256, 256)...]
where the time goes in v5:
time: 71 us; the launch traced here: 70.8 us
  Pallas kernels  70.1 us (99%)
    pallas_call x1, Pallas kernels, network_call(): pl.pallas_call(network, out_shape=(jax.ShapeDtypeStruct((UNITS, 256, 256)...  67.3 us
    pallas_call x1, Pallas kernels, per_device(): pl.pallas_call(widen, out_shape=(jax.ShapeDtypeStruct((1, 16, 32, 256), B...  2.85 us

profile of v5, /device:TPU:1, one launch (start us, length us, event | category | flops | bytes accessed | tf_op | source)
XLA Modules:
  0.0 70.8 jit_solution(3424145587196399589)
XLA Ops:
  0.6 67.3 %shard_map.84 = (bf16[12,256,256]{2,1,0:T(8,128)(2,1)}, bf16[16,32,256]{2,1,0:T(8,128)(2,1)}) custom-call(bf16[32,64,128]{2,1,0:T(8,128)(2,1)} %bitcast.2, bf16[3,3,128,128]{3,2,1,0:T(8,128)(2,1)} %k1_in.1, bf16[128,256]{1,0:T(8,128)(2,1)} %proj_in.1, bf16[3,3,256,256]{3,2,1,0:T(8,128)(2,1)} %k2_in.1, bf16[16,32,256]{2,1,0:T(8,128)(2,1)} %bitcast.3), custom_call_target="tpu_custom_call" | custom-call | flops 4000000000 | bytes 8388608 | tf_op jit(solution)/shard_map/pallas_call | solution.py:478
  67.9 2.8 %shard_map.85 = (bf16[1,16,32,256]{3,2,1,0:T(8,128)(2,1)}, f32[3,3,128,128]{3,2,1,0:T(8,128)}, f32[128,256]{1,0:T(8,128)}, f32[3,3,256,256]{3,2,1,0:T(8,128)}) custom-call(bf16[12,256,256]{2,1,0:T(8,128)(2,1)} %get-tuple-element.6.total, bf16[16,32,256]{2,1,0:T(8,128)(2,1)} %get-tuple-element.7.near), custom_call_target="tpu_custom_call" | custom-call | tf_op jit(solution)/shard_map/pallas_call | solution.py:556
